TPU v7x, 32 devices: a whole 2x2x4 slice. The times are simulated.
32 devices in a mesh: groups: 2 (over y), phi: 4 (over z), ev: 4 (over x, core).
Axes of the slice: x: 2, y: 2, z: 4, core: 2. Of those that a mesh axis runs over, the one named last changes fastest.
Arguments:
- cell_feats: bfloat16 [8, 1024, 256], P(('groups', 'ev'), 'phi'), parts along dimension 0, may hold values from -3 to 3
- neighbours: int32 [8, 8, 4], P(('groups', 'ev'), 'phi'), parts along dimension 0, may hold values from 0 to 3
- member_cell: int32 [8, 512], P(('groups', 'ev'), 'phi'), parts along dimension 0, may hold values from 0 to 255, as said below
- member_jet: int32 [8, 512, 1], P(('groups', 'ev'), 'phi'), parts along dimension 0, may hold values from 0 to 15, as said below
- cotangent: bfloat16 [8, 1024, 256], P(('groups', 'ev'), 'phi'), parts along dimension 0, may hold values from -3 to 3
- message_weight: bfloat16 [256, 256], replicated, may hold values from -0.375 to 0.375
- query_weight: bfloat16 [256, 256], replicated, may hold values from -4 to 4
- key_weight: bfloat16 [256, 256], replicated, may hold values from -4 to 4
- value_weight: bfloat16 [256, 256], replicated, may hold values from -0.375 to 0.375
- output_weight: bfloat16 [256, 256], replicated, may hold values from -0.375 to 0.375
Outputs:
- out_cells: bfloat16 [8, 1024, 256], P(('groups', 'ev'), 'phi'), parts along dimension 0
- grad_cells: bfloat16 [8, 1024, 256], P(('groups', 'ev'), 'phi'), parts along dimension 0
- grad_message: float32 [512, 256], P('groups'), parts along dimension 0
- grad_query: float32 [512, 256], P('groups'), parts along dimension 0
- grad_key: float32 [512, 256], P('groups'), parts along dimension 0
- grad_value: float32 [512, 256], P('groups'), parts along dimension 0
- grad_output: float32 [512, 256], P('groups'), parts along dimension 0
There are 2 independent parts, one for each index of `groups`. A program takes and returns all parts, laid end to end along the dimension named above; an argument that names none is the same for every part. Nothing has to cross between parts.
Inputs may be any that keep to these rules, and one draw needn't show every extreme that they name: `member_cell`: within one sector's 128 constituents of an event the cells are distinct. `member_jet`: A constituent of sector p belongs to a jet owned by one of the sectors p - 1 to p + 1 on the loop (jet j is owned by sector j // 4). Among one sector's 128 constituents of an event at most 21 belong to one jet, and some jet has exactly 21 of them.
All inputs are finite; a program needn't handle non-finite values.
Results may differ from a plain program's by a relative error of at most 0.0065.
The roundings to bfloat16 on the way count: a program that leaves them out, or rounds other values in their place, can miss the bound.
Values may be sent and summed in bfloat16 or wider, within the bound.
A program may use at most 64 MiB of HBM per device.

v0:
```python
import math

import jax
import jax.numpy as jnp
from jax import lax
from jax.sharding import PartitionSpec as P

HEADS = 8
BLOCK = 128
NBRS = 4
JET_DEV = 4


def extended_2(cells, sides, width):
    for axis, dim in sides:
        count = lax.axis_size(axis)
        head = lax.slice_in_dim(cells, 0, width, axis=dim)
        tail = lax.slice_in_dim(cells, cells.shape[dim] - width, cells.shape[dim], axis=dim)
        cells = jnp.concatenate(
            [
                lax.ppermute(tail, axis, [(i, (i + 1) % count) for i in range(count)]),
                cells,
                lax.ppermute(head, axis, [((i + 1) % count, i) for i in range(count)]),
            ],
            axis=dim,
        )
    return cells


def shortened(value):
    return jax.tree.map(lambda a: a.astype(jnp.bfloat16) if a.dtype == jnp.float32 else a, value)


def passed_along(block, axis, distance):
    devices = range(lax.axis_size(axis))
    route = [((i - distance) % len(devices), i) for i in devices]
    return lax.ppermute(block, axis, route)


def silu_slope(values):
    sigmoid = jax.nn.sigmoid(values)
    return sigmoid * (1.0 + values * (1.0 - sigmoid))


def attend_forward(members, present, query_weight, key_weight, value_weight, output_weight):
    jet_count, slot_count, channels = members.shape
    head_size = channels // HEADS
    score_scale = 1.0 / math.sqrt(head_size)
    flat_members = members.reshape(jet_count * slot_count, channels)

    def project(weight):
        result = jnp.dot(flat_members, weight, preferred_element_type=jnp.float32)
        return result.astype(jnp.bfloat16).reshape(jet_count, slot_count, HEADS, head_size)

    queries = project(query_weight)
    keyed = project(key_weight)
    valued = project(value_weight)
    scores = jnp.einsum("jqnd,jknd->jnqk", queries, keyed, preferred_element_type=jnp.float32)
    scores = jnp.where(present[:, None, None, :] > 0.5, scores * score_scale, -1e30)
    largest = jnp.max(scores, axis=-1, keepdims=True)
    powers = jnp.exp(scores - largest)
    chances = powers / jnp.sum(powers, axis=-1, keepdims=True)
    chances_low = chances.astype(jnp.bfloat16)
    mixture = jnp.einsum("jnqk,jknd->jqnd", chances_low, valued, preferred_element_type=jnp.float32)
    mixture = mixture.astype(jnp.bfloat16).reshape(jet_count * slot_count, channels)
    attended = jnp.dot(mixture, output_weight, preferred_element_type=jnp.float32).astype(
        jnp.bfloat16
    )
    return (
        attended.reshape(jet_count, slot_count, channels),
        (queries, keyed, valued, chances, chances_low, mixture),
    )


def attend_backward(
    members, saved, upstream, query_weight, key_weight, value_weight, output_weight
):
    queries, keyed, valued, chances, chances_low, mixture = saved
    jet_count, slot_count, channels = members.shape
    head_size = channels // HEADS
    score_scale = 1.0 / math.sqrt(head_size)
    flat_members = members.reshape(jet_count * slot_count, channels)
    flat_upstream = upstream.reshape(jet_count * slot_count, channels)
    output_term = jnp.dot(mixture.T, flat_upstream, preferred_element_type=jnp.float32)
    grad_mix = jnp.dot(flat_upstream, output_weight.T, preferred_element_type=jnp.float32)
    grad_mix = grad_mix.astype(jnp.bfloat16).reshape(jet_count, slot_count, HEADS, head_size)
    grad_chances = jnp.einsum(
        "jqnd,jknd->jnqk", grad_mix, valued, preferred_element_type=jnp.float32
    )
    grad_vals = jnp.einsum(
        "jnqk,jqnd->jknd", chances_low, grad_mix, preferred_element_type=jnp.float32
    )
    grad_vals = grad_vals.astype(jnp.bfloat16)
    inner_sum = jnp.sum(chances * grad_chances, axis=-1, keepdims=True)
    grad_scores = (chances * (grad_chances - inner_sum) * score_scale).astype(jnp.bfloat16)
    grad_queries = jnp.einsum(
        "jnqk,jknd->jqnd", grad_scores, keyed, preferred_element_type=jnp.float32
    )
    grad_keys = jnp.einsum(
        "jnqk,jqnd->jknd", grad_scores, queries, preferred_element_type=jnp.float32
    )
    flat_queries = grad_queries.astype(jnp.bfloat16).reshape(jet_count * slot_count, channels)
    flat_keys = grad_keys.astype(jnp.bfloat16).reshape(jet_count * slot_count, channels)
    flat_vals = grad_vals.reshape(jet_count * slot_count, channels)
    query_term = jnp.dot(flat_members.T, flat_queries, preferred_element_type=jnp.float32)
    key_term = jnp.dot(flat_members.T, flat_keys, preferred_element_type=jnp.float32)
    value_term = jnp.dot(flat_members.T, flat_vals, preferred_element_type=jnp.float32)
    grad_members = jnp.dot(flat_queries, query_weight.T, preferred_element_type=jnp.float32)
    grad_members = grad_members + jnp.dot(
        flat_keys, key_weight.T, preferred_element_type=jnp.float32
    )
    grad_members = grad_members + jnp.dot(
        flat_vals, value_weight.T, preferred_element_type=jnp.float32
    )
    grad_members = grad_members.astype(jnp.bfloat16).reshape(jet_count, slot_count, channels)
    return (grad_members, (query_term, key_term, value_term, output_term))


def direct_route(entries, mover):
    radius = (len(entries) - 1) // 2
    routed = []
    for slot_index in range(len(entries)):
        if slot_index == radius:
            routed.append(entries[radius])
        else:
            routed.append(mover(entries[2 * radius - slot_index], radius - slot_index))
    return routed


def on_device(
    cell_feats,
    neighbours,
    member_cell,
    member_jet,
    cotangent,
    message_weight,
    query_weight,
    key_weight,
    value_weight,
    output_weight,
):
    events, per_device, channels = cell_feats.shape
    sectors = lax.axis_size("phi")
    sector = lax.axis_index("phi")
    blocks = per_device // BLOCK
    members_dev = member_cell.shape[1]
    radius = min(4, (sectors - 1) // 2)
    window = 2 * radius + 1
    capacity = max(2, 2 * members_dev // (JET_DEV * window))
    slot_count = window * capacity
    window_jets = window * JET_DEV
    tiles = cell_feats.reshape(events, blocks, BLOCK, channels)
    extended = extended_2(tiles, (("phi", 1),), 1)
    counts = jnp.sum(
        (neighbours[..., None] == jnp.arange(blocks + 2, dtype=jnp.int32)).astype(jnp.bfloat16),
        axis=2,
    )
    gathered = jnp.einsum(
        "ebj,ejch->ebch", counts, extended, preferred_element_type=jnp.float32
    ) * (1.0 / NBRS)
    flat_gathered = gathered.astype(jnp.bfloat16).reshape(events * per_device, channels)
    before_act = jnp.dot(flat_gathered, message_weight, preferred_element_type=jnp.float32)
    hidden = (
        cell_feats.reshape(-1, channels).astype(jnp.float32) + jax.nn.silu(before_act)
    ).astype(jnp.bfloat16)
    hidden = hidden.reshape(events, per_device, channels)
    jet_ids = member_jet[..., 0]
    owner = jet_ids // JET_DEV
    offset_slot = (owner - sector + radius + sectors) % sectors
    local_ids = offset_slot * JET_DEV + jet_ids % JET_DEV
    positions = jnp.arange(members_dev, dtype=jnp.int32)
    jet_match = local_ids[..., None] == jnp.arange(window_jets, dtype=jnp.int32)
    earlier = (positions[:, None] > positions[None, :]).astype(jnp.bfloat16)
    prior = jnp.einsum(
        "ik,ekj->eij", earlier, jet_match.astype(jnp.bfloat16), preferred_element_type=jnp.float32
    )
    ranks = jnp.sum(jnp.where(jet_match, prior, 0.0), axis=-1).astype(jnp.int32)
    targets = local_ids * capacity + ranks
    slot_ids = jnp.arange(window_jets * capacity, dtype=jnp.int32)
    occupant = (
        jnp.sum(jnp.where(targets[..., None] == slot_ids, positions[None, :, None] + 1, 0), axis=1)
        - 1
    )
    picked = jnp.where(occupant >= 0, occupant, members_dev)
    cell_ids = jnp.arange(per_device, dtype=jnp.int32)
    holder = (
        jnp.sum(
            jnp.where(member_cell[..., None] == cell_ids, positions[None, :, None] + 1, 0), axis=1
        )
        - 1
    )
    holder_pick = jnp.where(holder >= 0, holder, members_dev)

    def to_slots(source):
        chosen = jnp.take_along_axis(source, member_cell[..., None], axis=1)
        padded = jnp.concatenate([chosen, jnp.zeros((events, 1, channels), chosen.dtype)], axis=1)
        placed_rows = jnp.take_along_axis(padded, picked[..., None], axis=1)
        return placed_rows.reshape(events, window, JET_DEV, capacity, channels)

    def to_cells(arrived_rows):
        flattened = arrived_rows.reshape(events, window_jets * capacity, channels)
        returned = jnp.take_along_axis(flattened, targets[..., None], axis=1)
        padded = jnp.concatenate(
            [returned, jnp.zeros((events, 1, channels), returned.dtype)], axis=1
        )
        return jnp.take_along_axis(padded, holder_pick[..., None], axis=1)

    feature_slots = to_slots(hidden)
    grad_slots = to_slots(cotangent)
    mask_slots = (occupant >= 0).astype(jnp.bfloat16).reshape(events, window, JET_DEV, capacity)
    outgoing = [
        (feature_slots[:, slot_index], grad_slots[:, slot_index], mask_slots[:, slot_index])
        for slot_index in range(window)
    ]
    arrived = direct_route(
        outgoing,
        lambda bundle, distance: jax.tree.map(
            lambda part, own: part.astype(own.dtype),
            passed_along(shortened(bundle), "phi", distance),
            bundle,
        ),
    )
    members = jnp.stack([entry[0] for entry in arrived], axis=2).reshape(
        events * JET_DEV, slot_count, channels
    )
    upstream = jnp.stack([entry[1] for entry in arrived], axis=2).reshape(
        events * JET_DEV, slot_count, channels
    )
    present = jnp.stack([entry[2] for entry in arrived], axis=2).reshape(
        events * JET_DEV, slot_count
    )
    attended, saved = attend_forward(
        members, present, query_weight, key_weight, value_weight, output_weight
    )
    grad_members, weight_terms = attend_backward(
        members, saved, upstream, query_weight, key_weight, value_weight, output_weight
    )
    attended_view = attended.reshape(events, JET_DEV, window, capacity, channels)
    grad_view = grad_members.reshape(events, JET_DEV, window, capacity, channels)
    returning = [
        (attended_view[:, :, slot_index], grad_view[:, :, slot_index])
        for slot_index in range(window)
    ]
    delivered = direct_route(
        returning,
        lambda bundle, distance: jax.tree.map(
            lambda part, own: part.astype(own.dtype),
            passed_along(shortened(bundle), "phi", distance),
            bundle,
        ),
    )
    returned_out = jnp.stack([entry[0] for entry in delivered], axis=1)
    returned_grad = jnp.stack([entry[1] for entry in delivered], axis=1)
    out_cells = (hidden.astype(jnp.float32) + to_cells(returned_out).astype(jnp.float32)).astype(
        jnp.bfloat16
    )
    grad_hidden = cotangent.astype(jnp.float32) + to_cells(returned_grad).astype(jnp.float32)
    grad_before = (grad_hidden.reshape(-1, channels) * silu_slope(before_act)).astype(jnp.bfloat16)
    message_term = jnp.dot(flat_gathered.T, grad_before, preferred_element_type=jnp.float32)
    grad_gathered = jnp.dot(
        grad_before, message_weight.T, preferred_element_type=jnp.float32
    ).astype(jnp.bfloat16)
    grad_gathered = grad_gathered.reshape(events, blocks, BLOCK, channels)
    grad_extended = jnp.einsum(
        "ebj,ebch->ejch", counts, grad_gathered, preferred_element_type=jnp.float32
    ) * (1.0 / NBRS)
    grad_extended = grad_extended.astype(jnp.bfloat16)
    from_lower = passed_along(grad_extended[:, blocks + 1 :], "phi", 1)
    from_upper = passed_along(grad_extended[:, :1], "phi", -1)
    summed = grad_hidden.reshape(events, blocks, BLOCK, channels) + grad_extended[
        :, 1 : blocks + 1
    ].astype(jnp.float32)
    summed = summed + jnp.pad(
        from_lower.astype(jnp.float32), ((0, 0), (0, blocks - 1), (0, 0), (0, 0))
    )
    summed = summed + jnp.pad(
        from_upper.astype(jnp.float32), ((0, 0), (blocks - 1, 0), (0, 0), (0, 0))
    )
    grad_cells = summed.astype(jnp.bfloat16).reshape(events, per_device, channels)
    totals = lax.psum(
        (message_term, weight_terms[0], weight_terms[1], weight_terms[2], weight_terms[3]),
        ("phi", "ev"),
    )
    squares = jnp.sum(jnp.stack([jnp.sum(matrix * matrix) for matrix in totals]))
    bound = math.sqrt(5.0) * channels
    factor = bound / jnp.maximum(jnp.sqrt(squares), bound)
    return (
        out_cells,
        grad_cells,
        totals[0] * factor,
        totals[1] * factor,
        totals[2] * factor,
        totals[3] * factor,
        totals[4] * factor,
    )


def solution(mesh):
    in_specs = (
        P(("groups", "ev"), "phi", None),
        P(("groups", "ev"), "phi", None),
        P(("groups", "ev"), "phi"),
        P(("groups", "ev"), "phi", None),
        P(("groups", "ev"), "phi", None),
        P(),
        P(),
        P(),
        P(),
        P(),
    )
    out_specs = (
        P(("groups", "ev"), "phi", None),
        P(("groups", "ev"), "phi", None),
        P("groups", None),
        P("groups", None),
        P("groups", None),
        P("groups", None),
        P("groups", None),
    )
    return jax.shard_map(
        on_device, mesh=mesh, in_specs=in_specs, out_specs=out_specs, check_vma=False
    )
```

profile of v0, /device:TPU:1, one launch (start us, length us, event | category | flops | bytes accessed | tf_op | source)
XLA Modules:
  0.0 194.8 jit_solution(7533739546687173720)
XLA Ops:
  8.2 4.6 %fusion.41 = s32[252]{0:T(256)S(1)} fusion(s32[128]{0:T(128)S(1)} %iota_add_fusion, s32[128]{0:T(128)S(1)} %get-tuple-element.42), kind=kLoop, calls=%fused_computation.93 | loop fusion | flops 96516 | bytes 2032 | tf_op jit(solution)/shard_map/reduce_sum | solution.py:181
  12.9 2.2 %collective-permute-start.4 = (bf16[1,4,21]{2,1,0:T(4,128)(2,1)S(1)}, bf16[1,4,21]{2,1,0:T(4,128)(2,1)S(1)}, u32[]{:S(2)}, u32[]{:S(2)}) collective-permute-start(bf16[1,4,21]{2,1,0:T(4,128)(2,1)S(1)} %get-tuple-element.38), channel_id=1, source_target_pairs={{12,0},{0,4},{4,8},{8,12},{13,1},{1,5},{5,9},{9,13},{14,2},{2,6},{... | collective-permute-start | bytes 512 | tf_op jit(solution)/shard_map/ppermute | solution.py:37
  15.1 2.1 %collective-permute-start.5 = (bf16[1,4,21]{2,1,0:T(4,128)(2,1)S(1)}, bf16[1,4,21]{2,1,0:T(4,128)(2,1)S(1)}, u32[]{:S(2)}, u32[]{:S(2)}) collective-permute-start(bf16[1,4,21]{2,1,0:T(4,128)(2,1)S(1)} %get-tuple-element.39), channel_id=1, source_target_pairs={{4,0},{8,4},{12,8},{0,12},{5,1},{9,5},{13,9},{1,13},{6,2},{10,6},{... | collective-permute-start | bytes 512 | tf_op jit(solution)/shard_map/ppermute | solution.py:37
  17.2 1.0 copy.103
  18.5 3.3 %collective-permute-start.1 = (bf16[1,1,128,256]{3,1,2,0:T(2,128)(2,1)S(1)}, bf16[1,1,128,256]{3,1,2,0:T(2,128)(2,1)S(1)}, u32[]{:S(2)}, u32[]{:S(2)}) collective-permute-start(bf16[1,1,128,256]{3,1,2,0:T(2,128)(2,1)S(1)} %get-tuple-element.37), channel_id=1, source_target_pairs={{4,0},{8,4},{12,8},{0,12},{5,1},{9,5},{13,9},{1,13},{6,2},{10,6},{... | collective-permute-start | bytes 196616 | tf_op jit(solution)/shard_map/ppermute | solution.py:23
  22.8 0.8 gather_fusion.4
  24.8 0.9 copy-done.13
  25.9 0.8 gather_fusion
  26.9 1.1 gather_fusion.5
  28.1 1.1 gather_fusion.1
  29.5 3.3 %collective-permute-start.9 = (bf16[1,4,21,256]{3,2,1,0:T(8,128)(2,1)S(1)}, bf16[1,4,21,256]{3,2,1,0:T(8,128)(2,1)S(1)}, u32[]{:S(2)}, u32[]{:S(2)}) collective-permute-start(bf16[1,4,21,256]{3,2,1,0:T(8,128)(2,1)S(1)} %get-tuple-element.28), channel_id=1, source_target_pairs={{4,0},{8,4},{12,8},{0,12},{5,1},{9,5},{13,9},{1,13},{6,2},{10,6},{... | collective-permute-start | bytes 129032 | tf_op jit(solution)/shard_map/ppermute | solution.py:37
  32.8 3.3 %collective-permute-start.3 = (bf16[1,4,21,256]{3,2,1,0:T(8,128)(2,1)S(1)}, bf16[1,4,21,256]{3,2,1,0:T(8,128)(2,1)S(1)}, u32[]{:S(2)}, u32[]{:S(2)}) collective-permute-start(bf16[1,4,21,256]{3,2,1,0:T(8,128)(2,1)S(1)} %get-tuple-element.34), channel_id=1, source_target_pairs={{4,0},{8,4},{12,8},{0,12},{5,1},{9,5},{13,9},{1,13},{6,2},{10,6},{... | collective-permute-start | bytes 129032 | tf_op jit(solution)/shard_map/ppermute | solution.py:37
  40.5 0.9 reshape.620
  42.2 2.5 %fusion.73 = (f32[4,8,63]{2,1,0:T(8,128)S(1)}, f32[4,8,63,63]{2,3,1,0:T(8,128)}) fusion(pred[4,63]{1,0:T(4,128)(4,1)S(1)} %gt.32, bf16[4,63,8,32]{1,0,3,2:T(4,128)(2,1)S(1)} %reshape.621, bf16[4,63,8,32]{1,0,3,2:T(4,128)(2,1)} %reshape.620), kind=kOutput, calls=%fused_computation.171 | convolution fusion | flops 8636606 | bytes 774396 | tf_op jit(solution)/shard_map/sub | solution.py:61
  44.7 2.8 %fusion.10 = bf16[4,63,8,32]{1,3,2,0:T(8,128)(2,1)} fusion(f32[4,8,63,63]{2,3,1,0:T(8,128)S(1)} %fusion.31, bf16[4,63,8,32]{1,0,3,2:T(4,128)(2,1)S(1)} %reshape.621, f32[4,8,63,63]{2,3,1,0:T(8,128)} %get-tuple-element.52, f32[4,8,63]{2,1,0:T(8,128)S(1)} %get-tuple-element.51), kind=kOutput, calls=%fused_computation.23 | convolution fusion | flops 9084158 | bytes 1282176 | tf_op jit(solution)/shard_map/jnqk,jknd->jqnd/dot_general | solution.py:96
  47.5 2.9 %fusion.11 = bf16[4,63,8,32]{1,3,2,0:T(8,128)(2,1)} fusion(f32[4,8,63,63]{2,3,1,0:T(8,128)S(1)} %fusion.31, bf16[4,63,8,32]{1,0,3,2:T(4,128)(2,1)} %reshape.620, f32[4,8,63,63]{2,3,1,0:T(8,128)} %get-tuple-element.52, f32[4,8,63]{2,1,0:T(8,128)S(1)} %get-tuple-element.51), kind=kOutput, calls=%fused_computation.24 | convolution fusion | flops 9084158 | bytes 1282176 | tf_op jit(solution)/shard_map/jnqk,jqnd->jknd/dot_general | solution.py:99
  50.4 1.7 fusion.12
  52.8 0.9 fusion.83
  55.1 0.9 fusion.80
  57.9 3.3 %collective-permute-start.7 = (bf16[1,4,21,256]{3,2,1,0:T(8,128)(2,1)S(1)}, bf16[1,4,21,256]{3,2,1,0:T(8,128)(2,1)S(1)}, u32[]{:S(2)}, u32[]{:S(2)}) collective-permute-start(bf16[1,4,21,256]{3,2,1,0:T(8,128)(2,1)S(1)} %get-tuple-element.31), channel_id=1, source_target_pairs={{4,0},{8,4},{12,8},{0,12},{5,1},{9,5},{13,9},{1,13},{6,2},{10,6},{... | collective-permute-start | bytes 129032 | tf_op jit(solution)/shard_map/ppermute | solution.py:37
  61.1 0.9 fusion.82
  62.1 0.9 fusion.81
  63.6 3.3 %collective-permute-start.11 = (bf16[1,4,21,256]{3,2,1,0:T(8,128)(2,1)S(1)}, bf16[1,4,21,256]{3,2,1,0:T(8,128)(2,1)S(1)}, u32[]{:S(2)}, u32[]{:S(2)}) collective-permute-start(bf16[1,4,21,256]{3,2,1,0:T(8,128)(2,1)S(1)} %get-tuple-element.25), channel_id=1, source_target_pairs={{4,0},{8,4},{12,8},{0,12},{5,1},{9,5},{13,9},{1,13},{6,2},{10,6},{... | collective-permute-start | bytes 129032 | tf_op jit(solution)/shard_map/ppermute | solution.py:37
  66.9 1.5 collective-permute-done.10
  69.4 0.8 gather_fusion.6
  70.3 1.2 gather_fusion.7
  71.6 0.9 fusion.79
  72.8 1.2 gather_fusion.3
  74.5 3.4 %collective-permute-start.13 = (bf16[1,1,128,256]{3,2,1,0:T(8,128)(2,1)S(1)}, bf16[1,1,128,256]{3,2,1,0:T(8,128)(2,1)S(1)}, u32[]{:S(2)}, u32[]{:S(2)}) collective-permute-start(bf16[1,1,128,256]{3,2,1,0:T(8,128)(2,1)S(1)} %get-tuple-element.23), channel_id=1, source_target_pairs={{4,0},{8,4},{12,8},{0,12},{5,1},{9,5},{13,9},{1,13},{6,2},{10,6},{... | collective-permute-start | bytes 196616 | tf_op jit(solution)/shard_map/ppermute | solution.py:37
  78.7 0.9 collective-permute-done.12
  80.3 96.1 %all-reduce.9.cloned.1.call-done = (f32[256,256]{1,0:T(8,128)}, f32[256,256]{1,0:T(8,128)}, f32[256,256]{1,0:T(8,128)}, f32[256,256]{1,0:T(8,128)}, f32[256,256]{1,0:T(8,128)}) async-done(((f32[256,256]{1,0:T(8,128)}, f32[256,256]{1,0:T(8,128)}, f32[256,256]{1,0:T(8,128)}, f32[256,256]{1,0:T(8,128)}, f32[256,256]{1,0:T(8,128)}), (f32[256,256]{1,0:T(8,128)}, f32[256,256]{1,0:T(8,128)}, f32[256,256]{1,0:T(8,128)}, ...) | async-done | bytes 1310736 | tf_op jit(solution)/shard_map/psum | solution.py:280
  176.3 1.7 multiply_reduce_fusion.1
  (148 shorter events, 23.7 us)
Async XLA Ops:
  7.2 17.7 %copy-start = (bf16[256,256]{1,0:T(8,128)(2,1)S(1)}, bf16[256,256]{1,0:T(8,128)(2,1)}, u32[]{:S(2)}) copy-start(bf16[256,256]{1,0:T(8,128)(2,1)} %param.23) | copy-start | bytes 393220
  7.2 169.2 %all-reduce.9.cloned.1.call-start = ((), (), s32[]{:S(2)}) async-start(), calls=%async_computation | async-start | bytes 2621440 | tf_op jit(solution)/shard_map/psum | solution.py:280
  12.9 10.8 %collective-permute-start.4 = (bf16[1,4,21]{2,1,0:T(4,128)(2,1)S(1)}, bf16[1,4,21]{2,1,0:T(4,128)(2,1)S(1)}, u32[]{:S(2)}, u32[]{:S(2)}) collective-permute-start(bf16[1,4,21]{2,1,0:T(4,128)(2,1)S(1)} %get-tuple-element.38), channel_id=1, source_target_pairs={{12,0},{0,4},{4,8},{8,12},{13,1},{1,5},{5,9},{9,13},{14,2},{2,6},{... | collective-permute-start | bytes 512 | tf_op jit(solution)/shard_map/ppermute | solution.py:37
  15.1 8.6 %collective-permute-start.5 = (bf16[1,4,21]{2,1,0:T(4,128)(2,1)S(1)}, bf16[1,4,21]{2,1,0:T(4,128)(2,1)S(1)}, u32[]{:S(2)}, u32[]{:S(2)}) collective-permute-start(bf16[1,4,21]{2,1,0:T(4,128)(2,1)S(1)} %get-tuple-element.39), channel_id=1, source_target_pairs={{4,0},{8,4},{12,8},{0,12},{5,1},{9,5},{13,9},{1,13},{6,2},{10,6},{... | collective-permute-start | bytes 512 | tf_op jit(solution)/shard_map/ppermute | solution.py:37
  18.2 4.6 %copy-start.1 = (bf16[1,256,256]{2,1,0:T(8,128)(2,1)S(1)}, bf16[1,256,256]{2,1,0:T(8,128)(2,1)}, u32[]{:S(2)}) copy-start(bf16[1,256,256]{2,1,0:T(8,128)(2,1)} %param.22) | copy-start | bytes 393220
  18.4 3.3 %copy-start.15 = (s32[1,128]{1,0:T(1,128)S(1)}, s32[1,128]{1,0:T(1,128)}, u32[]{:S(2)}) copy-start(s32[1,128]{1,0:T(1,128)} %param.20) | copy-start | bytes 1540
  18.4 5.8 %collective-permute-start = (bf16[1,1,128,256]{3,1,2,0:T(2,128)(2,1)S(1)}, bf16[1,1,128,256]{3,1,2,0:T(2,128)(2,1)S(1)}, u32[]{:S(2)}, u32[]{:S(2)}) collective-permute-start(bf16[1,1,128,256]{3,1,2,0:T(2,128)(2,1)S(1)} %get-tuple-element.36), channel_id=1, source_target_pairs={{0,4},{4,8},{8,12},{12,0},{1,5},{5,9},{9,13},{13,1},{2,6},{6,10},{... | collective-permute-start | bytes 196616 | tf_op jit(solution)/shard_map/ppermute | solution.py:21
  18.5 5.8 %collective-permute-start.1 = (bf16[1,1,128,256]{3,1,2,0:T(2,128)(2,1)S(1)}, bf16[1,1,128,256]{3,1,2,0:T(2,128)(2,1)S(1)}, u32[]{:S(2)}, u32[]{:S(2)}) collective-permute-start(bf16[1,1,128,256]{3,1,2,0:T(2,128)(2,1)S(1)} %get-tuple-element.37), channel_id=1, source_target_pairs={{4,0},{8,4},{12,8},{0,12},{5,1},{9,5},{13,9},{1,13},{6,2},{10,6},{... | collective-permute-start | bytes 196616 | tf_op jit(solution)/shard_map/ppermute | solution.py:23
  21.8 0.7 copy-start.16
  24.8 0.9 copy-start.13
  29.4 6.7 %collective-permute-start.8 = (bf16[1,4,21,256]{3,2,1,0:T(8,128)(2,1)S(1)}, bf16[1,4,21,256]{3,2,1,0:T(8,128)(2,1)S(1)}, u32[]{:S(2)}, u32[]{:S(2)}) collective-permute-start(bf16[1,4,21,256]{3,2,1,0:T(8,128)(2,1)S(1)} %get-tuple-element.27), channel_id=1, source_target_pairs={{12,0},{0,4},{4,8},{8,12},{13,1},{1,5},{5,9},{9,13},{14,2},{2,6},{... | collective-permute-start | bytes 129032 | tf_op jit(solution)/shard_map/ppermute | solution.py:37
  29.5 6.7 %collective-permute-start.9 = (bf16[1,4,21,256]{3,2,1,0:T(8,128)(2,1)S(1)}, bf16[1,4,21,256]{3,2,1,0:T(8,128)(2,1)S(1)}, u32[]{:S(2)}, u32[]{:S(2)}) collective-permute-start(bf16[1,4,21,256]{3,2,1,0:T(8,128)(2,1)S(1)} %get-tuple-element.28), channel_id=1, source_target_pairs={{4,0},{8,4},{12,8},{0,12},{5,1},{9,5},{13,9},{1,13},{6,2},{10,6},{... | collective-permute-start | bytes 129032 | tf_op jit(solution)/shard_map/ppermute | solution.py:37
  32.8 5.3 %collective-permute-start.2 = (bf16[1,4,21,256]{3,2,1,0:T(8,128)(2,1)S(1)}, bf16[1,4,21,256]{3,2,1,0:T(8,128)(2,1)S(1)}, u32[]{:S(2)}, u32[]{:S(2)}) collective-permute-start(bf16[1,4,21,256]{3,2,1,0:T(8,128)(2,1)S(1)} %get-tuple-element.33), channel_id=1, source_target_pairs={{12,0},{0,4},{4,8},{8,12},{13,1},{1,5},{5,9},{9,13},{14,2},{2,6},{... | collective-permute-start | bytes 129032 | tf_op jit(solution)/shard_map/ppermute | solution.py:37
  32.8 5.2 %collective-permute-start.3 = (bf16[1,4,21,256]{3,2,1,0:T(8,128)(2,1)S(1)}, bf16[1,4,21,256]{3,2,1,0:T(8,128)(2,1)S(1)}, u32[]{:S(2)}, u32[]{:S(2)}) collective-permute-start(bf16[1,4,21,256]{3,2,1,0:T(8,128)(2,1)S(1)} %get-tuple-element.34), channel_id=1, source_target_pairs={{4,0},{8,4},{12,8},{0,12},{5,1},{9,5},{13,9},{1,13},{6,2},{10,6},{... | collective-permute-start | bytes 129032 | tf_op jit(solution)/shard_map/ppermute | solution.py:37
  36.2 0.9 copy-start.7
  38.1 0.9 copy-start.10
  39.3 0.9 copy-start.9
  40.5 0.9 copy-start.8
  50.4 1.7 copy-start.17
  53.7 0.9 copy-start.12
  56.0 0.9 copy-start.11
  57.8 9.0 %collective-permute-start.6 = (bf16[1,4,21,256]{3,2,1,0:T(8,128)(2,1)S(1)}, bf16[1,4,21,256]{3,2,1,0:T(8,128)(2,1)S(1)}, u32[]{:S(2)}, u32[]{:S(2)}) collective-permute-start(bf16[1,4,21,256]{3,2,1,0:T(8,128)(2,1)S(1)} %get-tuple-element.30), channel_id=1, source_target_pairs={{12,0},{0,4},{4,8},{8,12},{13,1},{1,5},{5,9},{9,13},{14,2},{2,6},{... | collective-permute-start | bytes 129032 | tf_op jit(solution)/shard_map/ppermute | solution.py:37
  57.9 9.0 %collective-permute-start.7 = (bf16[1,4,21,256]{3,2,1,0:T(8,128)(2,1)S(1)}, bf16[1,4,21,256]{3,2,1,0:T(8,128)(2,1)S(1)}, u32[]{:S(2)}, u32[]{:S(2)}) collective-permute-start(bf16[1,4,21,256]{3,2,1,0:T(8,128)(2,1)S(1)} %get-tuple-element.31), channel_id=1, source_target_pairs={{4,0},{8,4},{12,8},{0,12},{5,1},{9,5},{13,9},{1,13},{6,2},{10,6},{... | collective-permute-start | bytes 129032 | tf_op jit(solution)/shard_map/ppermute | solution.py:37
  63.5 4.9 %collective-permute-start.10 = (bf16[1,4,21,256]{3,2,1,0:T(8,128)(2,1)S(1)}, bf16[1,4,21,256]{3,2,1,0:T(8,128)(2,1)S(1)}, u32[]{:S(2)}, u32[]{:S(2)}) collective-permute-start(bf16[1,4,21,256]{3,2,1,0:T(8,128)(2,1)S(1)} %get-tuple-element.24), channel_id=1, source_target_pairs={{12,0},{0,4},{4,8},{8,12},{13,1},{1,5},{5,9},{9,13},{14,2},{2,6},{... | collective-permute-start | bytes 129032 | tf_op jit(solution)/shard_map/ppermute | solution.py:37
  63.6 4.8 %collective-permute-start.11 = (bf16[1,4,21,256]{3,2,1,0:T(8,128)(2,1)S(1)}, bf16[1,4,21,256]{3,2,1,0:T(8,128)(2,1)S(1)}, u32[]{:S(2)}, u32[]{:S(2)}) collective-permute-start(bf16[1,4,21,256]{3,2,1,0:T(8,128)(2,1)S(1)} %get-tuple-element.25), channel_id=1, source_target_pairs={{4,0},{8,4},{12,8},{0,12},{5,1},{9,5},{13,9},{1,13},{6,2},{10,6},{... | collective-permute-start | bytes 129032 | tf_op jit(solution)/shard_map/ppermute | solution.py:37
  74.5 5.1 %collective-permute-start.12 = (bf16[1,1,128,256]{3,2,1,0:T(8,128)(2,1)S(1)}, bf16[1,1,128,256]{3,2,1,0:T(8,128)(2,1)S(1)}, u32[]{:S(2)}, u32[]{:S(2)}) collective-permute-start(bf16[1,1,128,256]{3,2,1,0:T(8,128)(2,1)S(1)} %get-tuple-element.22), channel_id=1, source_target_pairs={{12,0},{0,4},{4,8},{8,12},{13,1},{1,5},{5,9},{9,13},{14,2},{2,6},{... | collective-permute-start | bytes 196616 | tf_op jit(solution)/shard_map/ppermute | solution.py:37
  74.5 5.0 %collective-permute-start.13 = (bf16[1,1,128,256]{3,2,1,0:T(8,128)(2,1)S(1)}, bf16[1,1,128,256]{3,2,1,0:T(8,128)(2,1)S(1)}, u32[]{:S(2)}, u32[]{:S(2)}) collective-permute-start(bf16[1,1,128,256]{3,2,1,0:T(8,128)(2,1)S(1)} %get-tuple-element.23), channel_id=1, source_target_pairs={{4,0},{8,4},{12,8},{0,12},{5,1},{9,5},{13,9},{1,13},{6,2},{10,6},{... | collective-permute-start | bytes 196616 | tf_op jit(solution)/shard_map/ppermute | solution.py:37
  176.3 1.7 copy-start.4
  176.3 2.4 %copy-start.5 = (f32[256,256]{1,0:T(8,128)S(1)}, f32[256,256]{1,0:T(8,128)}, u32[]{:S(2)}) copy-start(f32[256,256]{1,0:T(8,128)} %get-tuple-element.13) | copy-start | bytes 786436
  178.0 1.3 copy-start.6
  178.7 1.3 copy-start.2
  185.5 1.0 copy-start.3
  (1 other events, 0.7 us)
Sparse Core Ops, SparseCore 0:
  74.6 101.7 all-reduce.8
where the time goes:
time: 196 us; the launch traced here: 195 us
  waiting for transfers between devices  99.4 us (51%)
  starting transfers between devices  24.3 us (12%)
  local copies, waits for them, and re-layouts  19.7 us (10%)
  matrix products  18.4 us (9%)
  between operations  18.1 us (9%)
  other arithmetic  15 us (8%)
    psum x1, waiting for transfers between devices, on_device(): lax.psum((message_term, weight_terms[0], weight_terms[1], weight_terms[2]...  96.1 us
    ppermute x12, starting transfers between devices, passed_along(): return lax.ppermute(block, axis, route)  21 us
    unnamed x36, local copies, waits for them, and re-layouts  6.42 us
    reduce_sum x1, other arithmetic, on_device(): jnp.sum(jnp.where(targets[..., None] == slot_ids, positions[None, :, None...  4.57 us
    reduce_sum x5, other arithmetic, on_device(): jnp.sum(matrix * matrix)  4.34 us
  transfers between devices with their start and end apart: 15, of which 5 were waited for; matrix products, arithmetic and copies ran while one was open for 4% of the time, Pallas kernels for 0%

commit v1 on v0

v1 whole, which is shorter than its diff:
```python
import functools
import math

import jax
import jax.numpy as jnp
from jax import lax
from jax.experimental import pallas as pl
from jax.experimental.pallas import tpu as pltpu
from jax.sharding import PartitionSpec as P

HEADS = 8
BLOCK = 128
NBRS = 4
JET_DEV = 4
TERMS = 4
MESH = pl.DeviceIdType.MESH
BF16 = jnp.bfloat16
F32 = jnp.float32


def contract(a, b, dim_a, dim_b):
    return lax.dot_general(a, b, (((dim_a,), (dim_b,)), ((), ())), preferred_element_type=F32)


def nn(a, b):
    return contract(a, b, 1, 0)


def nt(a, b):
    return contract(a, b, 1, 1)


def tn(a, b):
    return contract(a, b, 0, 0)


def wrapped(value, count):
    value = jnp.where(value >= count, value - count, value)
    return jnp.where(value >= count, value - count, value)


def layer_kernel(
    plan,
    cells,
    nbrs,
    mcell,
    mjet,
    cot,
    wm,
    wq,
    wk,
    wv,
    wo,
    out_cells,
    grad_cells,
    grad_message,
    grad_query,
    grad_key,
    grad_value,
    grad_output,
    edge_in,
    gedge_out,
    gedge_in,
    feat_out,
    feat_in,
    up_out,
    up_in,
    cnt_out,
    cnt_in,
    att_out,
    att_in,
    gmem_out,
    gmem_in,
    send_sem,
    recv_sem,
    *sums,
):
    sectors, ev_count, radius, capacity, fused = plan
    window = 2 * radius + 1
    rows = JET_DEV * capacity
    slots = window * capacity
    per_device, channels = cells.shape[1:]
    blocks = per_device // BLOCK
    cons = mcell.shape[1]
    sector = lax.axis_index("phi")
    ev = lax.axis_index("ev")
    pending = []

    def sector_at(distance):
        return lax.rem(sector + (distance + sectors), sectors)

    def ev_at(distance):
        return lax.rem(ev + distance, ev_count)

    def send(src, dst, **target):
        index = len(pending)
        copy = pltpu.make_async_remote_copy(
            src_ref=src,
            dst_ref=dst,
            send_sem=send_sem.at[index],
            recv_sem=recv_sem.at[index],
            device_id=target,
            device_id_type=MESH,
        )
        copy.start()
        pending.append(copy)
        return copy

    if fused:
        greeted = [{"phi": sector_at(d)} for d in range(1, sectors)]
        greeted += [{"ev": ev_at(d)} for d in range(1, ev_count)]
    else:
        greeted = [{"phi": sector_at(d)} for d in range(-radius, radius + 1) if d]
    barrier = pltpu.get_barrier_semaphore()
    for target in greeted:
        pl.semaphore_signal(barrier, inc=1, device_id=target, device_id_type=MESH)
    pl.semaphore_wait(barrier, len(greeted))

    edges = [
        send(cells.at[0, pl.ds((blocks - 1) * BLOCK, BLOCK)], edge_in.at[0], phi=sector_at(1)),
        send(cells.at[0, pl.ds(0, BLOCK)], edge_in.at[1], phi=sector_at(-1)),
    ]

    jets = mjet[0]
    offset = wrapped((jets >> 2) - sector + (radius + sectors), sectors)
    local_col = offset * JET_DEV + (jets & (JET_DEV - 1))
    up = lax.broadcasted_iota(jnp.int32, (cons, cons), 0)
    across = lax.broadcasted_iota(jnp.int32, (cons, cons), 1)
    local_row = jnp.sum(jnp.where(up == across, local_col, 0), axis=0, keepdims=True)
    same = jnp.where((up < across) & (local_col == local_row), 1, 0)
    target_row = local_row * capacity + jnp.sum(same, axis=0, keepdims=True)
    cell_hot = jnp.where(
        lax.broadcasted_iota(jnp.int32, (per_device, cons), 0) == mcell[...], 1.0, 0.0
    ).astype(BF16)
    slot_hot = jnp.where(
        lax.broadcasted_iota(jnp.int32, (window * rows, cons), 0) == target_row, 1.0, 0.0
    ).astype(BF16)
    slot_cell = nt(slot_hot, cell_hot).astype(BF16)
    cell_slot = nt(cell_hot, slot_hot).astype(BF16)

    def to_slots(source, out_ref, in_ref):
        placed = nn(slot_cell, source).astype(BF16)
        copies = []
        for w in range(window):
            part = placed[w * rows : (w + 1) * rows]
            if w == radius:
                in_ref[w] = part
            else:
                out_ref[w] = part
                copies.append(
                    send(out_ref.at[w], in_ref.at[2 * radius - w], phi=sector_at(w - radius))
                )
        return copies

    local_jet = lax.broadcasted_iota(jnp.int32, (16, cons), 0)
    arriving = to_slots(cot[0], up_out, up_in)
    for w in range(window):
        hit = (local_jet + w * JET_DEV == local_row) & (local_jet < JET_DEV)
        total = jnp.sum(jnp.where(hit, 1.0, 0.0), axis=1, keepdims=True)
        total = jnp.broadcast_to(total, (16, 128)).astype(BF16)
        if w == radius:
            cnt_in[w] = total
        else:
            cnt_out[w] = total
            arriving.append(
                send(cnt_out.at[w], cnt_in.at[2 * radius - w], phi=sector_at(w - radius))
            )

    counts = [
        [
            sum(jnp.where(nbrs[0, b, k] == j, 1.0, 0.0) for k in range(NBRS)) * (1.0 / NBRS)
            for j in range(blocks + 2)
        ]
        for b in range(blocks)
    ]
    for copy in edges:
        copy.wait_recv()
    extended = [edge_in[0].astype(F32)]
    extended += [cells[0, b * BLOCK : (b + 1) * BLOCK].astype(F32) for b in range(blocks)]
    extended += [edge_in[1].astype(F32)]
    gathered = jnp.concatenate(
        [sum(counts[b][j] * extended[j] for j in range(blocks + 2)) for b in range(blocks)],
        axis=0,
    ).astype(BF16)
    before_act = nn(gathered, wm[...])
    sigmoid = 1.0 / (1.0 + jnp.exp(-before_act))
    hidden = (cells[0].astype(F32) + before_act * sigmoid).astype(BF16)
    slope = sigmoid * (1.0 + before_act * (1.0 - sigmoid))
    features = to_slots(hidden, feat_out, feat_in)

    def by_jet(in_ref):
        parts = [in_ref[v].astype(F32) for v in range(window)]
        return jnp.concatenate(
            [
                parts[v][j * capacity : (j + 1) * capacity]
                for j in range(JET_DEV)
                for v in range(window)
            ],
            axis=0,
        ).astype(BF16)

    def back(rows_by_jet, out_ref, in_ref):
        copies = []
        for v in [v for v in range(window) if v != radius] + [radius]:
            part = jnp.concatenate(
                [
                    rows_by_jet[j * slots + v * capacity : j * slots + (v + 1) * capacity]
                    for j in range(JET_DEV)
                ],
                axis=0,
            ).astype(BF16)
            if v == radius:
                in_ref[v] = part
            else:
                out_ref[v] = part
                copies.append(
                    send(out_ref.at[v], in_ref.at[2 * radius - v], phi=sector_at(v - radius))
                )
        return copies

    for copy in arriving:
        copy.wait_recv()
    upstream = by_jet(up_in)
    grad_mix = nt(upstream, wo[...])
    lane = lax.broadcasted_iota(jnp.int32, (1, slots), 1)
    held = [cnt_in[v].astype(F32) for v in range(window)]
    present = []
    for j in range(JET_DEV):
        limit = jnp.zeros((1, slots), F32)
        for v in range(window):
            inside = (lane >= v * capacity) & (lane < (v + 1) * capacity)
            limit = jnp.where(inside, held[v][j : j + 1, :slots] + float(v * capacity), limit)
        present.append(lane.astype(F32) < limit)

    for copy in features:
        copy.wait_recv()
    members = by_jet(feat_in)
    queries = nn(members, wq[...])
    keyed = nn(members, wk[...])
    valued = nn(members, wv[...])

    head_size = channels // HEADS
    score_scale = 1.0 / math.sqrt(head_size)
    feature = lax.broadcasted_iota(jnp.int32, (slots, channels), 1)
    in_head = [
        (feature >= h * head_size) & (feature < (h + 1) * head_size) for h in range(HEADS)
    ]

    def spread(block):
        return jnp.concatenate(
            [jnp.where(in_head[h], block, 0.0) for h in range(HEADS)], axis=0
        ).astype(BF16)

    def merged(block):
        result = block[:slots]
        for h in range(1, HEADS):
            result = jnp.where(in_head[h], block[h * slots : (h + 1) * slots], result)
        return result

    saved = []
    mixture = []
    for j in range(JET_DEV):
        own = slice(j * slots, (j + 1) * slots)
        query_heads = spread(queries[own])
        keys = keyed[own].astype(BF16)
        vals = valued[own].astype(BF16)
        scores = nt(query_heads, keys)
        scores = jnp.where(present[j], scores * score_scale, -1e30)
        powers = jnp.exp(scores - jnp.max(scores, axis=1, keepdims=True))
        chances = powers * (1.0 / jnp.sum(powers, axis=1, keepdims=True))
        chances_low = chances.astype(BF16)
        mixture.append(merged(nn(chances_low, vals)))
        saved.append((query_heads, keys, vals, chances, chances_low))
    mixture = jnp.concatenate(mixture, axis=0).astype(BF16)
    attended = back(nn(mixture, wo[...]), att_out, att_in)

    grad_queries, grad_keys, grad_vals = [], [], []
    for j in range(JET_DEV):
        own = slice(j * slots, (j + 1) * slots)
        query_heads, keys, vals, chances, chances_low = saved[j]
        mix_heads = spread(grad_mix[own])
        grad_chances = nt(mix_heads, vals)
        grad_vals.append(tn(chances_low, mix_heads))
        inner = jnp.sum(chances * grad_chances, axis=1, keepdims=True)
        grad_scores = (chances * (grad_chances - inner) * score_scale).astype(BF16)
        grad_queries.append(merged(nn(grad_scores, keys)))
        grad_keys.append(tn(grad_scores, query_heads))
    grad_queries = jnp.concatenate(grad_queries, axis=0).astype(BF16)
    grad_keys = jnp.concatenate(grad_keys, axis=0).astype(BF16)
    grad_vals = jnp.concatenate(grad_vals, axis=0).astype(BF16)
    grad_members = nt(grad_queries, wq[...]) + nt(grad_keys, wk[...]) + nt(grad_vals, wv[...])
    returned = back(grad_members, gmem_out, gmem_in)

    terms = [
        tn(members, grad_queries),
        tn(members, grad_keys),
        tn(members, grad_vals),
        tn(mixture, upstream),
    ]

    def put(values, ref):
        flat = ref.shape[2]
        for e in range(ev_count):
            for p in range(sectors):
                first = (e * sectors + p) * flat
                value = values[first // channels]
                first = first % channels
                ref[e, p] = value[first : first + flat].astype(BF16)

    def share_ev(buffers):
        whole, landed = buffers[:2]
        return [
            send(whole.at[ev_at(d)], landed.at[d], ev=ev_at(d)) for d in range(1, ev_count)
        ]

    def share_phi(buffers, copies):
        whole, landed, middle, landed_phi = buffers[:4]
        for copy in copies:
            copy.wait_recv()
        total = whole[ev].astype(F32)
        for d in range(1, ev_count):
            total = total + landed[d].astype(F32)
        middle[...] = total.astype(BF16)
        return [
            send(middle.at[sector_at(d)], landed_phi.at[d], phi=sector_at(d))
            for d in range(1, sectors)
        ]

    def collect_phi(buffers, copies):
        middle, landed_phi, final = buffers[2:]
        for copy in copies:
            copy.wait_recv()
        total = middle[sector].astype(F32)
        for d in range(1, sectors):
            total = total + landed_phi[d].astype(F32)
        final[ev, sector] = total.astype(BF16)
        return [
            send(final.at[ev, sector], final.at[ev, sector], phi=sector_at(d))
            for d in range(1, sectors)
        ]

    def collect_ev(buffers, copies):
        final = buffers[4]
        for copy in copies:
            copy.wait_recv()
        return [send(final.at[ev], final.at[ev], ev=ev_at(d)) for d in range(1, ev_count)]

    if fused:
        first, second = sums[:5], sums[5:]
        put(terms, first[0])
        first_copies = share_ev(first)

    for copy in attended:
        copy.wait_recv()
    all_rows = att_in[...].reshape(window * rows, channels)
    out_cells[0] = (hidden.astype(F32) + nn(cell_slot, all_rows)).astype(BF16)
    for copy in returned:
        copy.wait_recv()
    all_rows = gmem_in[...].reshape(window * rows, channels)
    grad_hidden = cot[0].astype(F32) + nn(cell_slot, all_rows)
    grad_before = (grad_hidden * slope).astype(BF16)
    grad_gathered = nt(grad_before, wm[...]).astype(BF16).astype(F32)
    parts = [grad_gathered[b * BLOCK : (b + 1) * BLOCK] for b in range(blocks)]
    grad_extended = [
        sum(counts[b][j] * parts[b] for b in range(blocks)).astype(BF16)
        for j in range(blocks + 2)
    ]
    gedge_out[0] = grad_extended[blocks + 1]
    gedge_out[1] = grad_extended[0]
    grad_edges = [
        send(gedge_out.at[0], gedge_in.at[0], phi=sector_at(1)),
        send(gedge_out.at[1], gedge_in.at[1], phi=sector_at(-1)),
    ]
    message_term = tn(gathered, grad_before)
    if fused:
        put([message_term], second[0])
        second_copies = share_ev(second)
        first_copies = share_phi(first, first_copies)
    for copy in grad_edges:
        copy.wait_recv()
    for b in range(blocks):
        own = slice(b * BLOCK, (b + 1) * BLOCK)
        block = grad_hidden[own] + grad_extended[b + 1].astype(F32)
        if b == 0:
            block = block + gedge_in[0].astype(F32)
        if b == blocks - 1:
            block = block + gedge_in[1].astype(F32)
        grad_cells[0, own] = block.astype(BF16)

    results = [grad_query, grad_key, grad_value, grad_output]
    if fused:
        second_copies = share_phi(second, second_copies)
        first_copies = collect_phi(first, first_copies)
        second_copies = collect_phi(second, second_copies)
        first_copies = collect_ev(first, first_copies)
        second_copies = collect_ev(second, second_copies)
        for copy in first_copies + second_copies:
            copy.wait_recv()
        squares = jnp.zeros((1, channels), F32)
        for final in (first[4], second[4]):
            flat = final.shape[2]
            for e in range(ev_count):
                for p in range(sectors):
                    value = final[e, p].astype(F32)
                    squares = squares + jnp.sum(value * value, axis=0, keepdims=True)
        squares = jnp.sum(squares, axis=1, keepdims=True)
        bound = math.sqrt(5.0) * channels
        factor = bound / jnp.maximum(jnp.sqrt(squares), bound)
        for final, targets in ((first[4], results), (second[4], [grad_message])):
            flat = final.shape[2]
            for e in range(ev_count):
                for p in range(sectors):
                    start = (e * sectors + p) * flat
                    target = targets[start // channels]
                    start = start % channels
                    target[start : start + flat] = final[e, p].astype(F32) * factor
    else:
        for target, term in zip(results, terms):
            target[...] = term
        grad_message[...] = message_term
    for copy in pending:
        copy.wait_send()


def on_device(sectors, ev_count, *args):
    cell_feats, member_cell = args[0], args[2]
    per_device, channels = cell_feats.shape[1:]
    members_dev = member_cell.shape[1]
    radius = min(4, (sectors - 1) // 2)
    window = 2 * radius + 1
    capacity = max(2, 2 * members_dev // (JET_DEV * window))
    capacity = -(-capacity // 8) * 8
    rows = JET_DEV * capacity
    shares = sectors * ev_count
    fused = channels % (16 * shares) == 0
    copies = 4 + 5 * (window - 1)
    scratch = [pltpu.VMEM((2, BLOCK, channels), BF16) for _ in range(3)]
    scratch += [pltpu.VMEM((window, rows, channels), BF16) for _ in range(4)]
    scratch += [pltpu.VMEM((window, 16, 128), BF16) for _ in range(2)]
    scratch += [pltpu.VMEM((window, rows, channels), BF16) for _ in range(4)]
    sums = []
    if fused:
        copies += 4 * (ev_count - 1) + 4 * (sectors - 1)
        for count in (TERMS, 1):
            flat = count * channels // shares
            sums += [
                pltpu.VMEM((ev_count, sectors, flat, channels), BF16),
                pltpu.VMEM((ev_count, sectors, flat, channels), BF16),
                pltpu.VMEM((sectors, flat, channels), BF16),
                pltpu.VMEM((sectors, flat, channels), BF16),
                pltpu.VMEM((ev_count, sectors, flat, channels), BF16),
            ]
    scratch += [pltpu.SemaphoreType.DMA((copies,)), pltpu.SemaphoreType.DMA((copies,))]
    scratch += sums
    vmem = pl.BlockSpec(memory_space=pltpu.VMEM)
    in_specs = [vmem] * len(args)
    in_specs[1] = pl.BlockSpec(memory_space=pltpu.SMEM)
    cells_out = jax.ShapeDtypeStruct(cell_feats.shape, BF16)
    weight_out = jax.ShapeDtypeStruct((channels, channels), F32)
    outs = pl.pallas_call(
        functools.partial(
            layer_kernel, (sectors, ev_count, radius, capacity, fused)
        ),
        out_shape=[cells_out] * 2 + [weight_out] * 5,
        in_specs=in_specs,
        out_specs=[vmem] * 7,
        scratch_shapes=scratch,
        compiler_params=pltpu.CompilerParams(
            collective_id=0, has_side_effects=True, vmem_limit_bytes=48 * 1024 * 1024
        ),
        name="layer",
    )(*args)
    if fused:
        return tuple(outs)
    totals = lax.psum(tuple(outs[2:]), ("phi", "ev"))
    squares = sum(jnp.sum(matrix * matrix) for matrix in totals)
    bound = math.sqrt(5.0) * channels
    factor = bound / jnp.maximum(jnp.sqrt(squares), bound)
    return tuple(outs[:2]) + tuple(total * factor for total in totals)


def solution(mesh):
    cells = P(("groups", "ev"), "phi", None)
    in_specs = (cells, cells, P(("groups", "ev"), "phi"), cells, cells) + (P(),) * 5
    out_specs = (cells, cells) + (P("groups", None),) * 5
    return jax.shard_map(
        functools.partial(on_device, mesh.shape["phi"], mesh.shape["ev"]),
        mesh=mesh,
        in_specs=in_specs,
        out_specs=out_specs,
        check_vma=False,
    )
```

time: 196 us -> 57.2 us (0.29)
  waiting for transfers between devices: 99.4 us -> 0 us
  Pallas kernels: 0 us -> 44.1 us
  starting transfers between devices: 24.3 us -> 0 us
  matrix products: 18.4 us -> 0 us
  between operations: 18.1 us -> 0.69 us
  other arithmetic: 15 us -> 0 us
  local copies, waits for them, and re-layouts: 19.7 us -> 11.9 us
    psum x1 -> x0, waiting for transfers between devices: 96.1 us -> none  [on_device(): lax.psum((message_term, weight_terms[0], weight_terms[1], weight_terms[2]...]
    pallas_call x0 -> x1, Pallas kernels: none -> 44.1 us  [on_device(): pl.pallas_call(functools.partial(layer_kernel, (sectors, ev_count, radius...]
    ppermute x14 -> x0, starting transfers between devices: 24.3 us -> none  [the longest x12 21 us: passed_along(): return lax.ppermute(block, axis, route)]
    dot_general x23 -> x0, matrix products: 15.8 us -> none  [the longest x1 2.88 us: attend_backward(): jnp.einsum('jnqk,jqnd->jknd', grad_scores, queries, preferred_element_typ...]
    reduce_sum x8 -> x0, other arithmetic: 9.1 us -> none  [the longest x1 4.57 us: on_device(): jnp.sum(jnp.where(targets[..., None] == slot_ids, positions[None, :, None...]
    gather x8 -> x0, local copies, waits for them, and re-layouts: 7.98 us -> none  [the longest x2 2.3 us: to_cells(): return jnp.take_along_axis(padded, holder_pick[..., None], axis=1)]
    unnamed x36 -> x26, local copies, waits for them, and re-layouts: 6.42 us -> 11.9 us
    mul x5 -> x0, other arithmetic: 3.6 us -> none  [the longest x1 0.72 us: on_device(): totals[1] * factor]
  transfers between devices with their start and end apart: 15 -> 0, of which waited for: 5 -> 0; matrix products, arithmetic and copies ran while one was open for 4% -> 0% of each run, Pallas kernels for 0% -> 0%
where the time goes in v1:
time: 57.2 us; the launch traced here: 56.7 us
  Pallas kernels  44.1 us (77%)
  local copies, waits for them, and re-layouts  11.9 us (21%)
  between operations  0.69 us (1%)
    pallas_call x1, Pallas kernels, on_device(): pl.pallas_call(functools.partial(layer_kernel, (sectors, ev_count, radius...  44.1 us
    unnamed x26, local copies, waits for them, and re-layouts  11.9 us

profile of v1, /device:TPU:1, one launch (start us, length us, event | category | flops | bytes accessed | tf_op | source)
XLA Modules:
  0.0 56.7 jit_solution(3534311092630272612)
XLA Ops:
  0.6 0.0 copy-start.8
  0.6 0.0 copy-start.7
  0.7 0.8 %copy.17.mjet = s32[1,128,1]{2,1,0:T(8,128)S(1)} copy(s32[1,128,1]{1,2,0:T(1,128)} %param.13) | data formatting | bytes 1024 | tf_op args[3]
  1.4 0.0 copy-done.8
  1.4 0.0 copy-done.7
  1.4 0.0 copy-start
  1.5 0.9 %copy-done = bf16[1,256,256]{2,1,0:T(8,128)(2,1)S(1)} copy-done((bf16[1,256,256]{2,1,0:T(8,128)(2,1)S(1)}, bf16[1,256,256]{2,1,0:T(8,128)(2,1)}, u32[]{:S(2)}) %copy-start) | copy-done | bytes 131096
  2.3 0.0 copy-start.1
  2.4 0.9 %copy-done.1 = bf16[1,256,256]{2,1,0:T(8,128)(2,1)S(1)} copy-done((bf16[1,256,256]{2,1,0:T(8,128)(2,1)S(1)}, bf16[1,256,256]{2,1,0:T(8,128)(2,1)}, u32[]{:S(2)}) %copy-start.1) | copy-done | bytes 131096
  3.3 0.0 copy-start.2
  3.3 0.9 %copy-done.2 = bf16[256,256]{1,0:T(8,128)(2,1)S(1)} copy-done((bf16[256,256]{1,0:T(8,128)(2,1)S(1)}, bf16[256,256]{1,0:T(8,128)(2,1)}, u32[]{:S(2)}) %copy-start.2) | copy-done | bytes 131096
  4.2 0.0 copy-start.3
  4.2 0.9 %copy-done.3 = bf16[256,256]{1,0:T(8,128)(2,1)S(1)} copy-done((bf16[256,256]{1,0:T(8,128)(2,1)S(1)}, bf16[256,256]{1,0:T(8,128)(2,1)}, u32[]{:S(2)}) %copy-start.3) | copy-done | bytes 131096
  5.1 0.0 copy-start.4
  5.1 0.9 %copy-done.4 = bf16[256,256]{1,0:T(8,128)(2,1)S(1)} copy-done((bf16[256,256]{1,0:T(8,128)(2,1)S(1)}, bf16[256,256]{1,0:T(8,128)(2,1)}, u32[]{:S(2)}) %copy-start.4) | copy-done | bytes 131096
  6.0 0.0 copy-start.5
  6.0 0.9 %copy-done.5 = bf16[256,256]{1,0:T(8,128)(2,1)S(1)} copy-done((bf16[256,256]{1,0:T(8,128)(2,1)S(1)}, bf16[256,256]{1,0:T(8,128)(2,1)}, u32[]{:S(2)}) %copy-start.5) | copy-done | bytes 131096
  6.9 0.0 copy-start.6
  6.9 0.9 %copy-done.6 = bf16[256,256]{1,0:T(8,128)(2,1)S(1)} copy-done((bf16[256,256]{1,0:T(8,128)(2,1)S(1)}, bf16[256,256]{1,0:T(8,128)(2,1)}, u32[]{:S(2)}) %copy-start.6) | copy-done | bytes 131096
  7.8 44.1 %layer.1 = (bf16[1,256,256]{2,1,0:T(8,128)(2,1)S(1)}, bf16[1,256,256]{2,1,0:T(8,128)(2,1)S(1)}, f32[256,256]{1,0:T(8,128)S(1)}, f32[256,256]{1,0:T(8,128)S(1)}, ...) custom-call(bf16[1,256,256]{2,1,0:T(8,128)(2,1)S(1)} %copy-done, s32[1,2,4]{2,1,0:T(2,128)S(1)} %copy-done.7, ...), custom_call_target="tpu_custom_call" | custom-call | tf_op jit(solution)/shard_map/layer/pallas_call | solution.py:460
  51.8 0.7 %copy.25 = bf16[1,256,256]{2,1,0:T(8,128)(2,1)} copy(bf16[1,256,256]{2,1,0:T(8,128)(2,1)S(1)} %get-tuple-element.14) | data formatting | bytes 262144
  52.5 0.7 %copy.26 = bf16[1,256,256]{2,1,0:T(8,128)(2,1)} copy(bf16[1,256,256]{2,1,0:T(8,128)(2,1)S(1)} %get-tuple-element.15) | data formatting | bytes 262144
  53.2 0.7 %copy.27 = f32[256,256]{1,0:T(8,128)} copy(f32[256,256]{1,0:T(8,128)S(1)} %get-tuple-element.16) | data formatting | bytes 524288
  53.9 0.7 %copy.28 = f32[256,256]{1,0:T(8,128)} copy(f32[256,256]{1,0:T(8,128)S(1)} %get-tuple-element.17) | data formatting | bytes 524288
  54.6 0.7 %copy.29 = f32[256,256]{1,0:T(8,128)} copy(f32[256,256]{1,0:T(8,128)S(1)} %get-tuple-element.18) | data formatting | bytes 524288
  55.3 0.7 %copy.30 = f32[256,256]{1,0:T(8,128)} copy(f32[256,256]{1,0:T(8,128)S(1)} %get-tuple-element.19) | data formatting | bytes 524288
  56.0 0.7 %copy.31 = f32[256,256]{1,0:T(8,128)} copy(f32[256,256]{1,0:T(8,128)S(1)} %get-tuple-element.20) | data formatting | bytes 524288
Async XLA Ops:
  0.6 0.8 %copy-start.8 = (s32[1,128]{1,0:T(1,128)S(1)}, s32[1,128]{1,0:T(1,128)}, u32[]{:S(2)}) copy-start(s32[1,128]{1,0:T(1,128)} %mcell.1) | copy-start | bytes 1540
  0.6 0.8 %copy-start.7 = (s32[1,2,4]{2,1,0:T(2,128)S(1)}, s32[1,2,4]{2,1,0:T(2,128)}, u32[]{:S(2)}) copy-start(s32[1,2,4]{2,1,0:T(2,128)} %nbrs.1) | copy-start | bytes 100
  1.4 0.9 %copy-start = (bf16[1,256,256]{2,1,0:T(8,128)(2,1)S(1)}, bf16[1,256,256]{2,1,0:T(8,128)(2,1)}, u32[]{:S(2)}) copy-start(bf16[1,256,256]{2,1,0:T(8,128)(2,1)} %cells.1) | copy-start | bytes 393220
  2.3 0.9 %copy-start.1 = (bf16[1,256,256]{2,1,0:T(8,128)(2,1)S(1)}, bf16[1,256,256]{2,1,0:T(8,128)(2,1)}, u32[]{:S(2)}) copy-start(bf16[1,256,256]{2,1,0:T(8,128)(2,1)} %cot.1) | copy-start | bytes 393220
  3.3 0.9 %copy-start.2 = (bf16[256,256]{1,0:T(8,128)(2,1)S(1)}, bf16[256,256]{1,0:T(8,128)(2,1)}, u32[]{:S(2)}) copy-start(bf16[256,256]{1,0:T(8,128)(2,1)} %wm.1) | copy-start | bytes 393220
  4.2 0.9 %copy-start.3 = (bf16[256,256]{1,0:T(8,128)(2,1)S(1)}, bf16[256,256]{1,0:T(8,128)(2,1)}, u32[]{:S(2)}) copy-start(bf16[256,256]{1,0:T(8,128)(2,1)} %wq.1) | copy-start | bytes 393220
  5.1 0.9 %copy-start.4 = (bf16[256,256]{1,0:T(8,128)(2,1)S(1)}, bf16[256,256]{1,0:T(8,128)(2,1)}, u32[]{:S(2)}) copy-start(bf16[256,256]{1,0:T(8,128)(2,1)} %wk.1) | copy-start | bytes 393220
  6.0 0.9 %copy-start.5 = (bf16[256,256]{1,0:T(8,128)(2,1)S(1)}, bf16[256,256]{1,0:T(8,128)(2,1)}, u32[]{:S(2)}) copy-start(bf16[256,256]{1,0:T(8,128)(2,1)} %wv.1) | copy-start | bytes 393220
  6.9 0.9 %copy-start.6 = (bf16[256,256]{1,0:T(8,128)(2,1)S(1)}, bf16[256,256]{1,0:T(8,128)(2,1)}, u32[]{:S(2)}) copy-start(bf16[256,256]{1,0:T(8,128)(2,1)} %wo.1) | copy-start | bytes 393220

commit v2 on v1

--- a/solution.py
+++ b/solution.py
@@ -12,7 +12,7 @@
 BLOCK = 128
 NBRS = 4
 JET_DEV = 4
-TERMS = 4
+STORES = 4
 MESH = pl.DeviceIdType.MESH
 BF16 = jnp.bfloat16
 F32 = jnp.float32
@@ -41,16 +41,16 @@
 
 def layer_kernel(
     plan,
-    cells,
-    nbrs,
-    mcell,
-    mjet,
-    cot,
-    wm,
-    wq,
-    wk,
-    wv,
-    wo,
+    cells_far,
+    nbrs_far,
+    mcell_far,
+    mjet_far,
+    cot_far,
+    wm_far,
+    wq_far,
+    wk_far,
+    wv_far,
+    wo_far,
     out_cells,
     grad_cells,
     grad_message,
@@ -58,6 +58,17 @@
     grad_key,
     grad_value,
     grad_output,
+    cells,
+    cot,
+    wm,
+    wq,
+    wk,
+    wv,
+    wo,
+    nbrs,
+    mcell,
+    mjet,
+    load_sem,
     edge_in,
     gedge_out,
     gedge_in,
@@ -84,13 +95,30 @@
     cons = mcell.shape[1]
     sector = lax.axis_index("phi")
     ev = lax.axis_index("ev")
+    low, high = lax.rem(ev, 2), ev // 2
+    low_peer = ev + 1 - 2 * low
+    high_peer = ev + 2 - 4 * high
     pending = []
+
+    fetches = {}
+    fetched = (
+        ("mjet", mjet_far, mjet),
+        ("mcell", mcell_far, mcell),
+        ("nbrs", nbrs_far, nbrs),
+        ("cot", cot_far, cot),
+        ("cells", cells_far, cells),
+        ("wm", wm_far, wm),
+        ("wo", wo_far, wo),
+        ("wq", wq_far, wq),
+        ("wk", wk_far, wk),
+        ("wv", wv_far, wv),
+    )
+    for index, (name, far, near) in enumerate(fetched):
+        fetches[name] = pltpu.make_async_copy(far, near, load_sem.at[index])
+        fetches[name].start()
 
     def sector_at(distance):
         return lax.rem(sector + (distance + sectors), sectors)
-
-    def ev_at(distance):
-        return lax.rem(ev + distance, ev_count)
 
     def send(src, dst, **target):
         index = len(pending)
@@ -108,7 +136,8 @@
 
     if fused:
         greeted = [{"phi": sector_at(d)} for d in range(1, sectors)]
-        greeted += [{"ev": ev_at(d)} for d in range(1, ev_count)]
+        greeted += [{"phi": sector_at(d), "ev": high_peer} for d in range(sectors)]
+        greeted += [{"ev": low_peer}]
     else:
         greeted = [{"phi": sector_at(d)} for d in range(-radius, radius + 1) if d]
     barrier = pltpu.get_barrier_semaphore()
@@ -117,16 +146,18 @@
     pl.semaphore_wait(barrier, len(greeted))
 
     edges = [
-        send(cells.at[0, pl.ds((blocks - 1) * BLOCK, BLOCK)], edge_in.at[0], phi=sector_at(1)),
-        send(cells.at[0, pl.ds(0, BLOCK)], edge_in.at[1], phi=sector_at(-1)),
+        send(cells_far.at[0, pl.ds((blocks - 1) * BLOCK, BLOCK)], edge_in.at[0], phi=sector_at(1)),
+        send(cells_far.at[0, pl.ds(0, BLOCK)], edge_in.at[1], phi=sector_at(-1)),
     ]
 
-    jets = mjet[0]
+    for name in ("mjet", "mcell", "nbrs", "cot"):
+        fetches[name].wait()
+    jets = mjet[...]
     offset = wrapped((jets >> 2) - sector + (radius + sectors), sectors)
-    local_col = offset * JET_DEV + (jets & (JET_DEV - 1))
+    local_row = offset * JET_DEV + (jets & (JET_DEV - 1))
     up = lax.broadcasted_iota(jnp.int32, (cons, cons), 0)
     across = lax.broadcasted_iota(jnp.int32, (cons, cons), 1)
-    local_row = jnp.sum(jnp.where(up == across, local_col, 0), axis=0, keepdims=True)
+    local_col = jnp.sum(jnp.where(up == across, local_row, 0), axis=1, keepdims=True)
     same = jnp.where((up < across) & (local_col == local_row), 1, 0)
     target_row = local_row * capacity + jnp.sum(same, axis=0, keepdims=True)
     cell_hot = jnp.where(
@@ -168,11 +199,13 @@
 
     counts = [
         [
-            sum(jnp.where(nbrs[0, b, k] == j, 1.0, 0.0) for k in range(NBRS)) * (1.0 / NBRS)
+            jnp.sum(jnp.where(nbrs[0, b : b + 1] == j, 1.0 / NBRS, 0.0), axis=1, keepdims=True)
             for j in range(blocks + 2)
         ]
         for b in range(blocks)
     ]
+    for name in ("cells", "wm", "wo", "wq", "wk", "wv"):
+        fetches[name].wait()
     for copy in edges:
         copy.wait_recv()
     extended = [edge_in[0].astype(F32)]
@@ -274,81 +307,120 @@
     mixture = jnp.concatenate(mixture, axis=0).astype(BF16)
     attended = back(nn(mixture, wo[...]), att_out, att_in)
 
-    grad_queries, grad_keys, grad_vals = [], [], []
+    def put(values, buffers):
+        ref = buffers[0]
+        flat = ref.shape[3]
+        for c in range(2):
+            for x in range(2):
+                for p in range(sectors):
+                    first = ((c * 2 + x) * sectors + p) * flat
+                    value = values[first // channels]
+                    first = first % channels
+                    ref[c, x, p] = value[first : first + flat].astype(BF16)
+        return [send(ref.at[1 - low], buffers[1], ev=low_peer)]
+
+    def landed(copies):
+        for copy in copies:
+            copy.wait_recv()
+
+    def half(buffers, copies):
+        whole, from_low, middle, from_high = buffers[:4]
+        landed(copies)
+        middle[...] = (whole[low].astype(F32) + from_low[...].astype(F32)).astype(BF16)
+        return [send(middle.at[1 - high], from_high, ev=high_peer)]
+
+    def quarter(buffers, copies):
+        middle, from_high, share, from_phi = buffers[2:6]
+        landed(copies)
+        share[...] = (middle[high].astype(F32) + from_high[...].astype(F32)).astype(BF16)
+        return [
+            send(share.at[sector_at(d)], from_phi.at[d - 1], phi=sector_at(d))
+            for d in range(1, sectors)
+        ]
+
+    def own_total(buffers, copies):
+        share, from_phi, final = buffers[4:]
+        landed(copies)
+        total = share[sector].astype(F32)
+        for d in range(1, sectors):
+            total = total + from_phi[d - 1].astype(F32)
+        final[low, high, sector] = total.astype(BF16)
+        block = final.at[low, high, sector]
+        return [send(block, block, phi=sector_at(d)) for d in range(1, sectors)]
+
+    def chips():
+        for d in range(1, sectors):
+            yield d - 1, sector_at(d), ev, high
+        for d in range(sectors):
+            yield sectors - 1 + d, sector_at(d), high_peer, 1 - high
+
+    def direct(buffers, copies):
+        whole, from_low, middle, from_chips = buffers[:4]
+        landed(copies)
+        middle[...] = (whole[low].astype(F32) + from_low[...].astype(F32)).astype(BF16)
+        return [
+            send(middle.at[far_high, far], from_chips.at[index], phi=far, ev=far_ev)
+            for index, far, far_ev, far_high in chips()
+        ]
+
+    def direct_total(buffers, copies):
+        middle, from_chips, final = buffers[2:]
+        landed(copies)
+        total = middle[high, sector].astype(F32)
+        for index in range(2 * sectors - 1):
+            total = total + from_chips[index].astype(F32)
+        final[low, high, sector] = total.astype(BF16)
+        block = final.at[low, high, sector]
+        return [send(block, block, phi=far, ev=far_ev) for _, far, far_ev, _ in chips()]
+
+    def redouble_last(buffers, copies):
+        landed(copies)
+        block = buffers[4].at[low]
+        return [send(block, block, ev=low_peer)]
+
+    def double(buffers, copies):
+        landed(copies)
+        block = buffers[6].at[low, high]
+        return [send(block, block, ev=high_peer)]
+
+    def redouble(buffers, copies):
+        landed(copies)
+        block = buffers[6].at[low]
+        return [send(block, block, ev=low_peer)]
+
+    if fused:
+        early, late, last = sums[:7], sums[7:14], sums[14:]
+
+    mix_heads = [spread(grad_mix[j * slots : (j + 1) * slots]) for j in range(JET_DEV)]
+    grad_vals = jnp.concatenate(
+        [tn(saved[j][4], mix_heads[j]) for j in range(JET_DEV)], axis=0
+    ).astype(BF16)
+    value_term = tn(members, grad_vals)
+    output_term = tn(mixture, upstream)
+    if fused:
+        early_copies = put([value_term, output_term], early)
+
+    grad_queries, grad_keys = [], []
     for j in range(JET_DEV):
-        own = slice(j * slots, (j + 1) * slots)
         query_heads, keys, vals, chances, chances_low = saved[j]
-        mix_heads = spread(grad_mix[own])
-        grad_chances = nt(mix_heads, vals)
-        grad_vals.append(tn(chances_low, mix_heads))
+        grad_chances = nt(mix_heads[j], vals)
         inner = jnp.sum(chances * grad_chances, axis=1, keepdims=True)
         grad_scores = (chances * (grad_chances - inner) * score_scale).astype(BF16)
         grad_queries.append(merged(nn(grad_scores, keys)))
         grad_keys.append(tn(grad_scores, query_heads))
     grad_queries = jnp.concatenate(grad_queries, axis=0).astype(BF16)
     grad_keys = jnp.concatenate(grad_keys, axis=0).astype(BF16)
-    grad_vals = jnp.concatenate(grad_vals, axis=0).astype(BF16)
     grad_members = nt(grad_queries, wq[...]) + nt(grad_keys, wk[...]) + nt(grad_vals, wv[...])
     returned = back(grad_members, gmem_out, gmem_in)
-
-    terms = [
-        tn(members, grad_queries),
-        tn(members, grad_keys),
-        tn(members, grad_vals),
-        tn(mixture, upstream),
-    ]
-
-    def put(values, ref):
-        flat = ref.shape[2]
-        for e in range(ev_count):
-            for p in range(sectors):
-                first = (e * sectors + p) * flat
-                value = values[first // channels]
-                first = first % channels
-                ref[e, p] = value[first : first + flat].astype(BF16)
-
-    def share_ev(buffers):
-        whole, landed = buffers[:2]
-        return [
-            send(whole.at[ev_at(d)], landed.at[d], ev=ev_at(d)) for d in range(1, ev_count)
-        ]
-
-    def share_phi(buffers, copies):
-        whole, landed, middle, landed_phi = buffers[:4]
-        for copy in copies:
-            copy.wait_recv()
-        total = whole[ev].astype(F32)
-        for d in range(1, ev_count):
-            total = total + landed[d].astype(F32)
-        middle[...] = total.astype(BF16)
-        return [
-            send(middle.at[sector_at(d)], landed_phi.at[d], phi=sector_at(d))
-            for d in range(1, sectors)
-        ]
-
-    def collect_phi(buffers, copies):
-        middle, landed_phi, final = buffers[2:]
-        for copy in copies:
-            copy.wait_recv()
-        total = middle[sector].astype(F32)
-        for d in range(1, sectors):
-            total = total + landed_phi[d].astype(F32)
-        final[ev, sector] = total.astype(BF16)
-        return [
-            send(final.at[ev, sector], final.at[ev, sector], phi=sector_at(d))
-            for d in range(1, sectors)
-        ]
-
-    def collect_ev(buffers, copies):
-        final = buffers[4]
-        for copy in copies:
-            copy.wait_recv()
-        return [send(final.at[ev], final.at[ev], ev=ev_at(d)) for d in range(1, ev_count)]
-
-    if fused:
-        first, second = sums[:5], sums[5:]
-        put(terms, first[0])
-        first_copies = share_ev(first)
+    if fused:
+        early_copies = half(early, early_copies)
+
+    query_term = tn(members, grad_queries)
+    key_term = tn(members, grad_keys)
+    if fused:
+        late_copies = put([query_term, key_term], late)
+        early_copies = quarter(early, early_copies)
+        late_copies = half(late, late_copies)
 
     for copy in attended:
         copy.wait_recv()
@@ -359,6 +431,9 @@
     all_rows = gmem_in[...].reshape(window * rows, channels)
     grad_hidden = cot[0].astype(F32) + nn(cell_slot, all_rows)
     grad_before = (grad_hidden * slope).astype(BF16)
+    message_term = tn(gathered, grad_before)
+    if fused:
+        last_copies = put([message_term], last)
     grad_gathered = nt(grad_before, wm[...]).astype(BF16).astype(F32)
     parts = [grad_gathered[b * BLOCK : (b + 1) * BLOCK] for b in range(blocks)]
     grad_extended = [
@@ -371,11 +446,13 @@
         send(gedge_out.at[0], gedge_in.at[0], phi=sector_at(1)),
         send(gedge_out.at[1], gedge_in.at[1], phi=sector_at(-1)),
     ]
-    message_term = tn(gathered, grad_before)
-    if fused:
-        put([message_term], second[0])
-        second_copies = share_ev(second)
-        first_copies = share_phi(first, first_copies)
+    if fused:
+        early_copies = own_total(early, early_copies)
+        last_copies = direct(last, last_copies)
+        late_copies = quarter(late, late_copies)
+        early_copies = double(early, early_copies)
+        last_copies = direct_total(last, last_copies)
+        late_copies = own_total(late, late_copies)
     for copy in grad_edges:
         copy.wait_recv()
     for b in range(blocks):
@@ -387,39 +464,56 @@
             block = block + gedge_in[1].astype(F32)
         grad_cells[0, own] = block.astype(BF16)
 
-    results = [grad_query, grad_key, grad_value, grad_output]
-    if fused:
-        second_copies = share_phi(second, second_copies)
-        first_copies = collect_phi(first, first_copies)
-        second_copies = collect_phi(second, second_copies)
-        first_copies = collect_ev(first, first_copies)
-        second_copies = collect_ev(second, second_copies)
-        for copy in first_copies + second_copies:
-            copy.wait_recv()
+    if fused:
+        early_copies = redouble(early, early_copies)
+        late_copies = double(late, late_copies)
+        last_copies = redouble_last(last, last_copies)
+        late_copies = redouble(late, late_copies)
+        landed(early_copies + late_copies + last_copies)
         squares = jnp.zeros((1, channels), F32)
-        for final in (first[4], second[4]):
-            flat = final.shape[2]
-            for e in range(ev_count):
-                for p in range(sectors):
-                    value = final[e, p].astype(F32)
-                    squares = squares + jnp.sum(value * value, axis=0, keepdims=True)
+        blocks_of = [(c, x, p) for c in range(2) for x in range(2) for p in range(sectors)]
+        for buffers in (early, late, last):
+            for place in blocks_of:
+                value = buffers[-1][place].astype(F32)
+                squares = squares + jnp.sum(value * value, axis=0, keepdims=True)
         squares = jnp.sum(squares, axis=1, keepdims=True)
         bound = math.sqrt(5.0) * channels
         factor = bound / jnp.maximum(jnp.sqrt(squares), bound)
-        for final, targets in ((first[4], results), (second[4], [grad_message])):
-            flat = final.shape[2]
-            for e in range(ev_count):
-                for p in range(sectors):
-                    start = (e * sectors + p) * flat
-                    target = targets[start // channels]
-                    start = start % channels
-                    target[start : start + flat] = final[e, p].astype(F32) * factor
+        for buffers, targets in (
+            (early, [grad_value, grad_output]),
+            (late, [grad_query, grad_key]),
+            (last, [grad_message]),
+        ):
+            flat = buffers[-1].shape[3]
+            for index, place in enumerate(blocks_of):
+                target = targets[index * flat // channels]
+                start = index * flat % channels
+                target[start : start + flat] = buffers[-1][place].astype(F32) * factor
     else:
-        for target, term in zip(results, terms):
-            target[...] = term
+        grad_value[...] = value_term
+        grad_output[...] = output_term
+        grad_query[...] = query_term
+        grad_key[...] = key_term
         grad_message[...] = message_term
     for copy in pending:
         copy.wait_send()
+
+
+def store_kernel(*refs):
+    sem = refs[-1]
+    copies = []
+    for index in range(7):
+        near, far = refs[index], refs[7 + index]
+        lead = (0,) * (len(near.shape) - 2)
+        step = near.shape[-2] // STORES
+        for piece in range(STORES):
+            place = lead + (pl.ds(piece * step, step),)
+            copies.append(
+                pltpu.make_async_copy(near.at[place], far.at[place], sem.at[index, piece])
+            )
+            copies[-1].start()
+    for copy in copies:
+        copy.wait()
 
 
 def on_device(sectors, ev_count, *args):
@@ -432,37 +526,46 @@
     capacity = -(-capacity // 8) * 8
     rows = JET_DEV * capacity
     shares = sectors * ev_count
-    fused = channels % (16 * shares) == 0
+    fused = ev_count == 4 and channels % (16 * shares) == 0
     copies = 4 + 5 * (window - 1)
-    scratch = [pltpu.VMEM((2, BLOCK, channels), BF16) for _ in range(3)]
+    weight = (channels, channels)
+    scratch = [pltpu.VMEM(cell_feats.shape, BF16) for _ in range(2)]
+    scratch += [pltpu.VMEM(weight, BF16) for _ in range(5)]
+    scratch += [pltpu.VMEM(args[1].shape, jnp.int32)]
+    scratch += [pltpu.VMEM(member_cell.shape, jnp.int32) for _ in range(2)]
+    scratch += [pltpu.SemaphoreType.DMA((10,))]
+    scratch += [pltpu.VMEM((2, BLOCK, channels), BF16) for _ in range(3)]
     scratch += [pltpu.VMEM((window, rows, channels), BF16) for _ in range(4)]
     scratch += [pltpu.VMEM((window, 16, 128), BF16) for _ in range(2)]
     scratch += [pltpu.VMEM((window, rows, channels), BF16) for _ in range(4)]
     sums = []
     if fused:
-        copies += 4 * (ev_count - 1) + 4 * (sectors - 1)
-        for count in (TERMS, 1):
+        copies += 2 * (4 + 2 * (sectors - 1)) + 2 + 2 * (2 * sectors - 1)
+        grouped = [(2, 2, sectors), (2, sectors), (2, sectors), (sectors,), (sectors,)]
+        grouped += [(sectors - 1,), (2, 2, sectors)]
+        alone = grouped[:3] + [(2 * sectors - 1,), (2, 2, sectors)]
+        for count, leads in ((2, grouped), (2, grouped), (1, alone)):
             flat = count * channels // shares
-            sums += [
-                pltpu.VMEM((ev_count, sectors, flat, channels), BF16),
-                pltpu.VMEM((ev_count, sectors, flat, channels), BF16),
-                pltpu.VMEM((sectors, flat, channels), BF16),
-                pltpu.VMEM((sectors, flat, channels), BF16),
-                pltpu.VMEM((ev_count, sectors, flat, channels), BF16),
-            ]
+            sums += [pltpu.VMEM(lead + (flat, channels), BF16) for lead in leads]
     scratch += [pltpu.SemaphoreType.DMA((copies,)), pltpu.SemaphoreType.DMA((copies,))]
     scratch += sums
     vmem = pl.BlockSpec(memory_space=pltpu.VMEM)
-    in_specs = [vmem] * len(args)
-    in_specs[1] = pl.BlockSpec(memory_space=pltpu.SMEM)
+    far = pl.BlockSpec(memory_space=pltpu.HBM)
+    args = list(args)
+    args[3] = args[3].reshape(member_cell.shape)
+    args = [pltpu.with_memory_space_constraint(arg, pltpu.HBM) for arg in args]
     cells_out = jax.ShapeDtypeStruct(cell_feats.shape, BF16)
     weight_out = jax.ShapeDtypeStruct((channels, channels), F32)
+
+    def near(out):
+        return pltpu.VMEM(out.shape, out.dtype) if fused else out
+
     outs = pl.pallas_call(
         functools.partial(
             layer_kernel, (sectors, ev_count, radius, capacity, fused)
         ),
-        out_shape=[cells_out] * 2 + [weight_out] * 5,
-        in_specs=in_specs,
+        out_shape=[near(cells_out)] * 2 + [near(weight_out)] * 5,
+        in_specs=[far] * len(args),
         out_specs=[vmem] * 7,
         scratch_shapes=scratch,
         compiler_params=pltpu.CompilerParams(
@@ -471,7 +574,17 @@
         name="layer",
     )(*args)
     if fused:
-        return tuple(outs)
+        outs = [pltpu.with_memory_space_constraint(out, pltpu.VMEM) for out in outs]
+        return tuple(
+            pl.pallas_call(
+                store_kernel,
+                out_shape=[jax.ShapeDtypeStruct(out.shape, out.dtype) for out in outs],
+                in_specs=[vmem] * 7,
+                out_specs=[far] * 7,
+                scratch_shapes=[pltpu.SemaphoreType.DMA((7, STORES))],
+                name="store",
+            )(*outs)
+        )
     totals = lax.psum(tuple(outs[2:]), ("phi", "ev"))
     squares = sum(jnp.sum(matrix * matrix) for matrix in totals)
     bound = math.sqrt(5.0) * channels

time: 57.2 us -> 47.4 us (0.83)
  local copies, waits for them, and re-layouts: 11.9 us -> 0 us
  Pallas kernels: 44.1 us -> 46.6 us
    unnamed x26 -> x0, local copies, waits for them, and re-layouts: 11.9 us -> none
    pallas_call x0 -> x1, Pallas kernels: none -> 1.37 us  [on_device(): pl.pallas_call(store_kernel, out_shape=[jax.ShapeDtypeStruct(out.shape, o...]
    pallas_call x1, Pallas kernels: 44.1 us -> 45.2 us  [on_device(): pl.pallas_call(functools.partial(layer_kernel, (sectors, ev_count, radius...]
where the time goes in v2:
time: 47.4 us; the launch traced here: 47.3 us
  Pallas kernels  46.6 us (98%)
  between operations  0.64 us (1%)
    pallas_call x1, Pallas kernels, on_device(): pl.pallas_call(functools.partial(layer_kernel, (sectors, ev_count, radius...  45.2 us
    pallas_call x1, Pallas kernels, on_device(): pl.pallas_call(store_kernel, out_shape=[jax.ShapeDtypeStruct(out.shape, o...  1.37 us

profile of v2, /device:TPU:1, one launch (start us, length us, event | category | flops | bytes accessed | tf_op | source)
XLA Modules:
  0.0 47.3 jit_solution(8326220298970874807)
XLA Ops:
  0.6 45.2 %layer.1 = (bf16[1,256,256]{2,1,0:T(8,128)(2,1)S(1)}, bf16[1,256,256]{2,1,0:T(8,128)(2,1)S(1)}, f32[256,256]{1,0:T(8,128)S(1)}, f32[256,256]{1,0:T(8,128)S(1)}, ...) custom-call(bf16[1,256,256]{2,1,0:T(8,128)(2,1)} %cells_far.1, s32[1,2,4]{2,1,0:T(2,128)} %nbrs_far.1, ...), custom_call_target="tpu_custom_call" | custom-call | tf_op jit(solution)/shard_map/layer/pallas_call | solution.py:563
  45.9 1.4 %store.1 = (bf16[1,256,256]{2,1,0:T(8,128)(2,1)}, bf16[1,256,256]{2,1,0:T(8,128)(2,1)}, f32[256,256]{1,0:T(8,128)}, f32[256,256]{1,0:T(8,128)}, f32[256,256]{1,0...) custom-call(bf16[1,256,256]{2,1,0:T(8,128)(2,1)S(1)} %get-tuple-element.14.refs_0_, ...), custom_call_target="tpu_custom_call" | custom-call | tf_op jit(solution)/shard_map/store/pallas_call | solution.py:579

commit v3 on v2

--- a/solution.py
+++ b/solution.py
@@ -82,6 +82,8 @@
     att_in,
     gmem_out,
     gmem_in,
+    gath_out,
+    gath_in,
     send_sem,
     recv_sem,
     *sums,
@@ -134,10 +136,13 @@
         pending.append(copy)
         return copy
 
+    def landed(copies):
+        for copy in copies:
+            copy.wait_recv()
+
     if fused:
         greeted = [{"phi": sector_at(d)} for d in range(1, sectors)]
-        greeted += [{"phi": sector_at(d), "ev": high_peer} for d in range(sectors)]
-        greeted += [{"ev": low_peer}]
+        greeted += [{"ev": high_peer}, {"ev": low_peer}]
     else:
         greeted = [{"phi": sector_at(d)} for d in range(-radius, radius + 1) if d]
     barrier = pltpu.get_barrier_semaphore()
@@ -184,7 +189,7 @@
         return copies
 
     local_jet = lax.broadcasted_iota(jnp.int32, (16, cons), 0)
-    arriving = to_slots(cot[0], up_out, up_in)
+    counted = []
     for w in range(window):
         hit = (local_jet + w * JET_DEV == local_row) & (local_jet < JET_DEV)
         total = jnp.sum(jnp.where(hit, 1.0, 0.0), axis=1, keepdims=True)
@@ -193,7 +198,7 @@
             cnt_in[w] = total
         else:
             cnt_out[w] = total
-            arriving.append(
+            counted.append(
                 send(cnt_out.at[w], cnt_in.at[2 * radius - w], phi=sector_at(w - radius))
             )
 
@@ -220,6 +225,12 @@
     hidden = (cells[0].astype(F32) + before_act * sigmoid).astype(BF16)
     slope = sigmoid * (1.0 + before_act * (1.0 - sigmoid))
     features = to_slots(hidden, feat_out, feat_in)
+    upstreams = to_slots(cot[0], up_out, up_in)
+    member_gathered = to_slots(gathered, gath_out, gath_in)
+
+    bare = jnp.sum(cell_hot.astype(F32), axis=1, keepdims=True) < 0.5
+    bare_grad = jnp.where(bare, cot[0].astype(F32) * slope, 0.0).astype(BF16)
+    bare_term = tn(gathered, bare_grad)
 
     def by_jet(in_ref):
         parts = [in_ref[v].astype(F32) for v in range(window)]
@@ -251,10 +262,7 @@
                 )
         return copies
 
-    for copy in arriving:
-        copy.wait_recv()
-    upstream = by_jet(up_in)
-    grad_mix = nt(upstream, wo[...])
+    landed(counted)
     lane = lax.broadcasted_iota(jnp.int32, (1, slots), 1)
     held = [cnt_in[v].astype(F32) for v in range(window)]
     present = []
@@ -265,8 +273,7 @@
             limit = jnp.where(inside, held[v][j : j + 1, :slots] + float(v * capacity), limit)
         present.append(lane.astype(F32) < limit)
 
-    for copy in features:
-        copy.wait_recv()
+    landed(features)
     members = by_jet(feat_in)
     queries = nn(members, wq[...])
     keyed = nn(members, wk[...])
@@ -307,90 +314,51 @@
     mixture = jnp.concatenate(mixture, axis=0).astype(BF16)
     attended = back(nn(mixture, wo[...]), att_out, att_in)
 
+    bits = [low, high, lax.rem(sector, 2), sector // 2]
+    peers = [
+        {"ev": low_peer},
+        {"ev": high_peer},
+        {"phi": sector + 1 - 2 * bits[2]},
+        {"phi": sector + 2 - 4 * bits[3]},
+    ]
+    shares = [(a, b, c, d) for a in range(2) for b in range(2) for c in range(2) for d in range(2)]
+
     def put(values, buffers):
         ref = buffers[0]
-        flat = ref.shape[3]
-        for c in range(2):
-            for x in range(2):
-                for p in range(sectors):
-                    first = ((c * 2 + x) * sectors + p) * flat
-                    value = values[first // channels]
-                    first = first % channels
-                    ref[c, x, p] = value[first : first + flat].astype(BF16)
-        return [send(ref.at[1 - low], buffers[1], ev=low_peer)]
-
-    def landed(copies):
-        for copy in copies:
-            copy.wait_recv()
-
-    def half(buffers, copies):
-        whole, from_low, middle, from_high = buffers[:4]
-        landed(copies)
-        middle[...] = (whole[low].astype(F32) + from_low[...].astype(F32)).astype(BF16)
-        return [send(middle.at[1 - high], from_high, ev=high_peer)]
-
-    def quarter(buffers, copies):
-        middle, from_high, share, from_phi = buffers[2:6]
-        landed(copies)
-        share[...] = (middle[high].astype(F32) + from_high[...].astype(F32)).astype(BF16)
-        return [
-            send(share.at[sector_at(d)], from_phi.at[d - 1], phi=sector_at(d))
-            for d in range(1, sectors)
-        ]
-
-    def own_total(buffers, copies):
-        share, from_phi, final = buffers[4:]
-        landed(copies)
-        total = share[sector].astype(F32)
-        for d in range(1, sectors):
-            total = total + from_phi[d - 1].astype(F32)
-        final[low, high, sector] = total.astype(BF16)
-        block = final.at[low, high, sector]
-        return [send(block, block, phi=sector_at(d)) for d in range(1, sectors)]
-
-    def chips():
-        for d in range(1, sectors):
-            yield d - 1, sector_at(d), ev, high
-        for d in range(sectors):
-            yield sectors - 1 + d, sector_at(d), high_peer, 1 - high
-
-    def direct(buffers, copies):
-        whole, from_low, middle, from_chips = buffers[:4]
-        landed(copies)
-        middle[...] = (whole[low].astype(F32) + from_low[...].astype(F32)).astype(BF16)
-        return [
-            send(middle.at[far_high, far], from_chips.at[index], phi=far, ev=far_ev)
-            for index, far, far_ev, far_high in chips()
-        ]
-
-    def direct_total(buffers, copies):
-        middle, from_chips, final = buffers[2:]
-        landed(copies)
-        total = middle[high, sector].astype(F32)
-        for index in range(2 * sectors - 1):
-            total = total + from_chips[index].astype(F32)
-        final[low, high, sector] = total.astype(BF16)
-        block = final.at[low, high, sector]
-        return [send(block, block, phi=far, ev=far_ev) for _, far, far_ev, _ in chips()]
-
-    def redouble_last(buffers, copies):
-        landed(copies)
-        block = buffers[4].at[low]
-        return [send(block, block, ev=low_peer)]
-
-    def double(buffers, copies):
-        landed(copies)
-        block = buffers[6].at[low, high]
-        return [send(block, block, ev=high_peer)]
-
-    def redouble(buffers, copies):
-        landed(copies)
-        block = buffers[6].at[low]
-        return [send(block, block, ev=low_peer)]
-
-    if fused:
-        early, late, last = sums[:7], sums[7:14], sums[14:]
-
+        flat = ref.shape[4]
+        for index, place in enumerate(shares):
+            first = index * flat
+            value = values[first // channels]
+            first = first % channels
+            ref[place] = value[first : first + flat].astype(BF16)
+        copies = [send(ref.at[1 - bits[0]], buffers[4], **peers[0])]
+        return {"buffers": buffers, "copies": copies, "step": 0}
+
+    def advance(group):
+        buffers, step = group["buffers"], group["step"]
+        landed(group["copies"])
+        final = buffers[8]
+        if step < 4:
+            total = buffers[step][bits[step]].astype(F32) + buffers[4 + step][...].astype(F32)
+        if step < 3:
+            held = buffers[step + 1]
+            held[...] = total.astype(BF16)
+            copy = send(
+                held.at[1 - bits[step + 1]], buffers[5 + step], **peers[step + 1]
+            )
+        else:
+            if step == 3:
+                final[tuple(bits)] = total.astype(BF16)
+            block = final.at[tuple(bits[: 7 - step])]
+            copy = send(block, block, **peers[6 - step])
+        group["copies"], group["step"] = [copy], step + 1
+
+    if fused:
+        early, late, last = sums[:9], sums[9:18], sums[18:]
+
+    landed(upstreams)
+    upstream = by_jet(up_in)
+    grad_mix = nt(upstream, wo[...])
     mix_heads = [spread(grad_mix[j * slots : (j + 1) * slots]) for j in range(JET_DEV)]
     grad_vals = jnp.concatenate(
         [tn(saved[j][4], mix_heads[j]) for j in range(JET_DEV)], axis=0
@@ -398,7 +366,7 @@
     value_term = tn(members, grad_vals)
     output_term = tn(mixture, upstream)
     if fused:
-        early_copies = put([value_term, output_term], early)
+        early = put([value_term, output_term], early)
 
     grad_queries, grad_keys = [], []
     for j in range(JET_DEV):
@@ -413,27 +381,34 @@
     grad_members = nt(grad_queries, wq[...]) + nt(grad_keys, wk[...]) + nt(grad_vals, wv[...])
     returned = back(grad_members, gmem_out, gmem_in)
     if fused:
-        early_copies = half(early, early_copies)
+        advance(early)
 
     query_term = tn(members, grad_queries)
     key_term = tn(members, grad_keys)
     if fused:
-        late_copies = put([query_term, key_term], late)
-        early_copies = quarter(early, early_copies)
-        late_copies = half(late, late_copies)
-
-    for copy in attended:
-        copy.wait_recv()
+        late = put([query_term, key_term], late)
+    landed(member_gathered)
+    rows_gathered = by_jet(gath_in)
+    rows_act = nn(rows_gathered, wm[...])
+    rows_sigmoid = 1.0 / (1.0 + jnp.exp(-rows_act))
+    rows_slope = rows_sigmoid * (1.0 + rows_act * (1.0 - rows_sigmoid))
+    rows_grad = upstream.astype(F32) + grad_members.astype(BF16).astype(F32)
+    message_term = bare_term + tn(rows_gathered, (rows_grad * rows_slope).astype(BF16))
+    if fused:
+        last = put([message_term], last)
+        for group in (early, late, last):
+            advance(group)
+
+    landed(attended)
     all_rows = att_in[...].reshape(window * rows, channels)
     out_cells[0] = (hidden.astype(F32) + nn(cell_slot, all_rows)).astype(BF16)
-    for copy in returned:
-        copy.wait_recv()
+    if fused:
+        for group in (early, late, last):
+            advance(group)
+    landed(returned)
     all_rows = gmem_in[...].reshape(window * rows, channels)
     grad_hidden = cot[0].astype(F32) + nn(cell_slot, all_rows)
     grad_before = (grad_hidden * slope).astype(BF16)
-    message_term = tn(gathered, grad_before)
-    if fused:
-        last_copies = put([message_term], last)
     grad_gathered = nt(grad_before, wm[...]).astype(BF16).astype(F32)
     parts = [grad_gathered[b * BLOCK : (b + 1) * BLOCK] for b in range(blocks)]
     grad_extended = [
@@ -447,14 +422,10 @@
         send(gedge_out.at[1], gedge_in.at[1], phi=sector_at(-1)),
     ]
     if fused:
-        early_copies = own_total(early, early_copies)
-        last_copies = direct(last, last_copies)
-        late_copies = quarter(late, late_copies)
-        early_copies = double(early, early_copies)
-        last_copies = direct_total(last, last_copies)
-        late_copies = own_total(late, late_copies)
-    for copy in grad_edges:
-        copy.wait_recv()
+        for _ in range(3):
+            for group in (early, late, last):
+                advance(group)
+    landed(grad_edges)
     for b in range(blocks):
         own = slice(b * BLOCK, (b + 1) * BLOCK)
         block = grad_hidden[own] + grad_extended[b + 1].astype(F32)
@@ -465,30 +436,28 @@
         grad_cells[0, own] = block.astype(BF16)
 
     if fused:
-        early_copies = redouble(early, early_copies)
-        late_copies = double(late, late_copies)
-        last_copies = redouble_last(last, last_copies)
-        late_copies = redouble(late, late_copies)
-        landed(early_copies + late_copies + last_copies)
+        advance(early)
+        for _ in range(2):
+            advance(late)
+            advance(last)
+        landed(early["copies"] + late["copies"] + last["copies"])
         squares = jnp.zeros((1, channels), F32)
-        blocks_of = [(c, x, p) for c in range(2) for x in range(2) for p in range(sectors)]
-        for buffers in (early, late, last):
-            for place in blocks_of:
-                value = buffers[-1][place].astype(F32)
+        groups = (early, late, last)
+        finals = [group["buffers"][8] for group in groups]
+        for final in finals:
+            for place in shares:
+                value = final[place].astype(F32)
                 squares = squares + jnp.sum(value * value, axis=0, keepdims=True)
         squares = jnp.sum(squares, axis=1, keepdims=True)
         bound = math.sqrt(5.0) * channels
         factor = bound / jnp.maximum(jnp.sqrt(squares), bound)
-        for buffers, targets in (
-            (early, [grad_value, grad_output]),
-            (late, [grad_query, grad_key]),
-            (last, [grad_message]),
-        ):
-            flat = buffers[-1].shape[3]
-            for index, place in enumerate(blocks_of):
-                target = targets[index * flat // channels]
+        targets = ([grad_value, grad_output], [grad_query, grad_key], [grad_message])
+        for final, whole in zip(finals, targets):
+            flat = final.shape[4]
+            for index, place in enumerate(shares):
+                target = whole[index * flat // channels]
                 start = index * flat % channels
-                target[start : start + flat] = buffers[-1][place].astype(F32) * factor
+                target[start : start + flat] = final[place].astype(F32) * factor
     else:
         grad_value[...] = value_term
         grad_output[...] = output_term
@@ -526,8 +495,8 @@
     capacity = -(-capacity // 8) * 8
     rows = JET_DEV * capacity
     shares = sectors * ev_count
-    fused = ev_count == 4 and channels % (16 * shares) == 0
-    copies = 4 + 5 * (window - 1)
+    fused = ev_count == 4 and sectors == 4 and channels % (16 * shares) == 0
+    copies = 4 + 6 * (window - 1)
     weight = (channels, channels)
     scratch = [pltpu.VMEM(cell_feats.shape, BF16) for _ in range(2)]
     scratch += [pltpu.VMEM(weight, BF16) for _ in range(5)]
@@ -537,14 +506,12 @@
     scratch += [pltpu.VMEM((2, BLOCK, channels), BF16) for _ in range(3)]
     scratch += [pltpu.VMEM((window, rows, channels), BF16) for _ in range(4)]
     scratch += [pltpu.VMEM((window, 16, 128), BF16) for _ in range(2)]
-    scratch += [pltpu.VMEM((window, rows, channels), BF16) for _ in range(4)]
+    scratch += [pltpu.VMEM((window, rows, channels), BF16) for _ in range(6)]
     sums = []
     if fused:
-        copies += 2 * (4 + 2 * (sectors - 1)) + 2 + 2 * (2 * sectors - 1)
-        grouped = [(2, 2, sectors), (2, sectors), (2, sectors), (sectors,), (sectors,)]
-        grouped += [(sectors - 1,), (2, 2, sectors)]
-        alone = grouped[:3] + [(2 * sectors - 1,), (2, 2, sectors)]
-        for count, leads in ((2, grouped), (2, grouped), (1, alone)):
+        copies += 3 * 8
+        leads = [(2,) * count for count in (4, 3, 2, 1, 3, 2, 1, 0, 4)]
+        for count in (2, 2, 1):
             flat = count * channels // shares
             sums += [pltpu.VMEM(lead + (flat, channels), BF16) for lead in leads]
     scratch += [pltpu.SemaphoreType.DMA((copies,)), pltpu.SemaphoreType.DMA((copies,))]

time: 47.4 us -> 50.9 us (1.074)
  Pallas kernels: 46.6 us -> 50.1 us
    pallas_call x1, Pallas kernels: 45.2 us -> 48.7 us  [on_device(): pl.pallas_call(functools.partial(layer_kernel, (sectors, ev_count, radius...]
where the time goes in v3:
time: 50.9 us; the launch traced here: 50.7 us
  Pallas kernels  50.1 us (98%)
  between operations  0.64 us (1%)
    pallas_call x1, Pallas kernels, on_device(): pl.pallas_call(functools.partial(layer_kernel, (sectors, ev_count, radius...  48.7 us
    pallas_call x1, Pallas kernels, on_device(): pl.pallas_call(store_kernel, out_shape=[jax.ShapeDtypeStruct(out.shape, o...  1.37 us

profile of v3, /device:TPU:1, one launch (start us, length us, event | category | flops | bytes accessed | tf_op | source)
XLA Modules:
  0.0 50.7 jit_solution(11489730020681944585)
XLA Ops:
  0.6 48.7 %layer.1 = (bf16[1,256,256]{2,1,0:T(8,128)(2,1)S(1)}, bf16[1,256,256]{2,1,0:T(8,128)(2,1)S(1)}, f32[256,256]{1,0:T(8,128)S(1)}, f32[256,256]{1,0:T(8,128)S(1)}, ...) custom-call(bf16[1,256,256]{2,1,0:T(8,128)(2,1)} %cells_far.1, s32[1,2,4]{2,1,0:T(2,128)} %nbrs_far.1, ...), custom_call_target="tpu_custom_call" | custom-call | tf_op jit(solution)/shard_map/layer/pallas_call | solution.py:530
  49.4 1.4 %store.1 = (bf16[1,256,256]{2,1,0:T(8,128)(2,1)}, bf16[1,256,256]{2,1,0:T(8,128)(2,1)}, f32[256,256]{1,0:T(8,128)}, f32[256,256]{1,0:T(8,128)}, f32[256,256]{1,0...) custom-call(bf16[1,256,256]{2,1,0:T(8,128)(2,1)S(1)} %get-tuple-element.14.refs_0_, ...), custom_call_target="tpu_custom_call" | custom-call | tf_op jit(solution)/shard_map/store/pallas_call | solution.py:546

commit v4 on v3

--- a/solution.py
+++ b/solution.py
@@ -97,9 +97,6 @@
     cons = mcell.shape[1]
     sector = lax.axis_index("phi")
     ev = lax.axis_index("ev")
-    low, high = lax.rem(ev, 2), ev // 2
-    low_peer = ev + 1 - 2 * low
-    high_peer = ev + 2 - 4 * high
     pending = []
 
     fetches = {}
@@ -122,6 +119,9 @@
     def sector_at(distance):
         return lax.rem(sector + (distance + sectors), sectors)
 
+    def ev_at(distance):
+        return lax.rem(ev + distance, ev_count)
+
     def send(src, dst, **target):
         index = len(pending)
         copy = pltpu.make_async_remote_copy(
@@ -142,7 +142,7 @@
 
     if fused:
         greeted = [{"phi": sector_at(d)} for d in range(1, sectors)]
-        greeted += [{"ev": high_peer}, {"ev": low_peer}]
+        greeted += [{"ev": ev_at(d)} for d in range(1, ev_count)]
     else:
         greeted = [{"phi": sector_at(d)} for d in range(-radius, radius + 1) if d]
     barrier = pltpu.get_barrier_semaphore()
@@ -314,47 +314,50 @@
     mixture = jnp.concatenate(mixture, axis=0).astype(BF16)
     attended = back(nn(mixture, wo[...]), att_out, att_in)
 
-    bits = [low, high, lax.rem(sector, 2), sector // 2]
-    peers = [
-        {"ev": low_peer},
-        {"ev": high_peer},
-        {"phi": sector + 1 - 2 * bits[2]},
-        {"phi": sector + 2 - 4 * bits[3]},
-    ]
-    shares = [(a, b, c, d) for a in range(2) for b in range(2) for c in range(2) for d in range(2)]
-
     def put(values, buffers):
         ref = buffers[0]
-        flat = ref.shape[4]
-        for index, place in enumerate(shares):
-            first = index * flat
-            value = values[first // channels]
-            first = first % channels
-            ref[place] = value[first : first + flat].astype(BF16)
-        copies = [send(ref.at[1 - bits[0]], buffers[4], **peers[0])]
-        return {"buffers": buffers, "copies": copies, "step": 0}
-
-    def advance(group):
-        buffers, step = group["buffers"], group["step"]
-        landed(group["copies"])
-        final = buffers[8]
-        if step < 4:
-            total = buffers[step][bits[step]].astype(F32) + buffers[4 + step][...].astype(F32)
-        if step < 3:
-            held = buffers[step + 1]
-            held[...] = total.astype(BF16)
-            copy = send(
-                held.at[1 - bits[step + 1]], buffers[5 + step], **peers[step + 1]
-            )
-        else:
-            if step == 3:
-                final[tuple(bits)] = total.astype(BF16)
-            block = final.at[tuple(bits[: 7 - step])]
-            copy = send(block, block, **peers[6 - step])
-        group["copies"], group["step"] = [copy], step + 1
-
-    if fused:
-        early, late, last = sums[:9], sums[9:18], sums[18:]
+        flat = ref.shape[2]
+        piece = math.gcd(flat, channels)
+        for e in range(ev_count):
+            for p in range(sectors):
+                for row in range(0, flat, piece):
+                    first = (e * sectors + p) * flat + row
+                    value = values[first // channels]
+                    first = first % channels
+                    ref[e, p, row : row + piece] = value[first : first + piece].astype(BF16)
+        return [
+            send(ref.at[ev_at(d)], buffers[1].at[d - 1], ev=ev_at(d)) for d in range(1, ev_count)
+        ]
+
+    def share_phi(buffers, copies):
+        whole, from_ev, middle, from_phi = buffers[:4]
+        landed(copies)
+        total = whole[ev].astype(F32)
+        for d in range(1, ev_count):
+            total = total + from_ev[d - 1].astype(F32)
+        middle[...] = total.astype(BF16)
+        return [
+            send(middle.at[sector_at(d)], from_phi.at[d - 1], phi=sector_at(d))
+            for d in range(1, sectors)
+        ]
+
+    def own_total(buffers, copies):
+        middle, from_phi, final = buffers[2:]
+        landed(copies)
+        total = middle[sector].astype(F32)
+        for d in range(1, sectors):
+            total = total + from_phi[d - 1].astype(F32)
+        final[ev, sector] = total.astype(BF16)
+        block = final.at[ev, sector]
+        return [send(block, block, phi=sector_at(d)) for d in range(1, sectors)]
+
+    def back_ev(buffers, copies):
+        landed(copies)
+        block = buffers[4].at[ev]
+        return [send(block, block, ev=ev_at(d)) for d in range(1, ev_count)]
+
+    if fused:
+        early, late = sums[:5], sums[5:]
 
     landed(upstreams)
     upstream = by_jet(up_in)
@@ -366,7 +369,7 @@
     value_term = tn(members, grad_vals)
     output_term = tn(mixture, upstream)
     if fused:
-        early = put([value_term, output_term], early)
+        early_copies = put([value_term, output_term], early)
 
     grad_queries, grad_keys = [], []
     for j in range(JET_DEV):
@@ -381,12 +384,10 @@
     grad_members = nt(grad_queries, wq[...]) + nt(grad_keys, wk[...]) + nt(grad_vals, wv[...])
     returned = back(grad_members, gmem_out, gmem_in)
     if fused:
-        advance(early)
+        early_copies = share_phi(early, early_copies)
 
     query_term = tn(members, grad_queries)
     key_term = tn(members, grad_keys)
-    if fused:
-        late = put([query_term, key_term], late)
     landed(member_gathered)
     rows_gathered = by_jet(gath_in)
     rows_act = nn(rows_gathered, wm[...])
@@ -395,16 +396,15 @@
     rows_grad = upstream.astype(F32) + grad_members.astype(BF16).astype(F32)
     message_term = bare_term + tn(rows_gathered, (rows_grad * rows_slope).astype(BF16))
     if fused:
-        last = put([message_term], last)
-        for group in (early, late, last):
-            advance(group)
+        late_copies = put([query_term, key_term, message_term], late)
+        early_copies = own_total(early, early_copies)
 
     landed(attended)
     all_rows = att_in[...].reshape(window * rows, channels)
     out_cells[0] = (hidden.astype(F32) + nn(cell_slot, all_rows)).astype(BF16)
     if fused:
-        for group in (early, late, last):
-            advance(group)
+        late_copies = share_phi(late, late_copies)
+        early_copies = back_ev(early, early_copies)
     landed(returned)
     all_rows = gmem_in[...].reshape(window * rows, channels)
     grad_hidden = cot[0].astype(F32) + nn(cell_slot, all_rows)
@@ -422,9 +422,7 @@
         send(gedge_out.at[1], gedge_in.at[1], phi=sector_at(-1)),
     ]
     if fused:
-        for _ in range(3):
-            for group in (early, late, last):
-                advance(group)
+        late_copies = own_total(late, late_copies)
     landed(grad_edges)
     for b in range(blocks):
         own = slice(b * BLOCK, (b + 1) * BLOCK)
@@ -436,28 +434,30 @@
         grad_cells[0, own] = block.astype(BF16)
 
     if fused:
-        advance(early)
-        for _ in range(2):
-            advance(late)
-            advance(last)
-        landed(early["copies"] + late["copies"] + last["copies"])
+        late_copies = back_ev(late, late_copies)
+        landed(early_copies + late_copies)
         squares = jnp.zeros((1, channels), F32)
-        groups = (early, late, last)
-        finals = [group["buffers"][8] for group in groups]
-        for final in finals:
-            for place in shares:
-                value = final[place].astype(F32)
+        blocks_of = [(e, p) for e in range(ev_count) for p in range(sectors)]
+        for buffers in (early, late):
+            for place in blocks_of:
+                value = buffers[-1][place].astype(F32)
                 squares = squares + jnp.sum(value * value, axis=0, keepdims=True)
         squares = jnp.sum(squares, axis=1, keepdims=True)
         bound = math.sqrt(5.0) * channels
         factor = bound / jnp.maximum(jnp.sqrt(squares), bound)
-        targets = ([grad_value, grad_output], [grad_query, grad_key], [grad_message])
-        for final, whole in zip(finals, targets):
-            flat = final.shape[4]
-            for index, place in enumerate(shares):
-                target = whole[index * flat // channels]
-                start = index * flat % channels
-                target[start : start + flat] = final[place].astype(F32) * factor
+        for buffers, targets in (
+            (early, [grad_value, grad_output]),
+            (late, [grad_query, grad_key, grad_message]),
+        ):
+            flat = buffers[-1].shape[2]
+            piece = math.gcd(flat, channels)
+            for index, place in enumerate(blocks_of):
+                block = buffers[-1][place].astype(F32) * factor
+                for row in range(0, flat, piece):
+                    start = index * flat + row
+                    target = targets[start // channels]
+                    start = start % channels
+                    target[start : start + piece] = block[row : row + piece]
     else:
         grad_value[...] = value_term
         grad_output[...] = output_term
@@ -495,7 +495,7 @@
     capacity = -(-capacity // 8) * 8
     rows = JET_DEV * capacity
     shares = sectors * ev_count
-    fused = ev_count == 4 and sectors == 4 and channels % (16 * shares) == 0
+    fused = channels % (16 * shares) == 0
     copies = 4 + 6 * (window - 1)
     weight = (channels, channels)
     scratch = [pltpu.VMEM(cell_feats.shape, BF16) for _ in range(2)]
@@ -509,9 +509,10 @@
     scratch += [pltpu.VMEM((window, rows, channels), BF16) for _ in range(6)]
     sums = []
     if fused:
-        copies += 3 * 8
-        leads = [(2,) * count for count in (4, 3, 2, 1, 3, 2, 1, 0, 4)]
-        for count in (2, 2, 1):
+        copies += 4 * (ev_count - 1) + 4 * (sectors - 1)
+        leads = [(ev_count, sectors), (ev_count - 1, sectors), (sectors,), (sectors - 1,)]
+        leads += [(ev_count, sectors)]
+        for count in (2, 3):
             flat = count * channels // shares
             sums += [pltpu.VMEM(lead + (flat, channels), BF16) for lead in leads]
     scratch += [pltpu.SemaphoreType.DMA((copies,)), pltpu.SemaphoreType.DMA((copies,))]

time: 50.9 us -> 47.4 us (0.931)
  Pallas kernels: 50.1 us -> 46.6 us
    pallas_call x1, Pallas kernels: 48.7 us -> 45.3 us  [on_device(): pl.pallas_call(functools.partial(layer_kernel, (sectors, ev_count, radius...]
where the time goes in v4:
time: 47.4 us; the launch traced here: 47.3 us
  Pallas kernels  46.6 us (98%)
  between operations  0.64 us (1%)
    pallas_call x1, Pallas kernels, on_device(): pl.pallas_call(functools.partial(layer_kernel, (sectors, ev_count, radius...  45.3 us
    pallas_call x1, Pallas kernels, on_device(): pl.pallas_call(store_kernel, out_shape=[jax.ShapeDtypeStruct(out.shape, o...  1.37 us

profile of v4, /device:TPU:1, one launch (start us, length us, event | category | flops | bytes accessed | tf_op | source)
XLA Modules:
  0.0 47.3 jit_solution(14627439194129160275)
XLA Ops:
  0.6 45.3 %layer.1 = (bf16[1,256,256]{2,1,0:T(8,128)(2,1)S(1)}, bf16[1,256,256]{2,1,0:T(8,128)(2,1)S(1)}, f32[256,256]{1,0:T(8,128)S(1)}, f32[256,256]{1,0:T(8,128)S(1)}, ...) custom-call(bf16[1,256,256]{2,1,0:T(8,128)(2,1)} %cells_far.1, s32[1,2,4]{2,1,0:T(2,128)} %nbrs_far.1, ...), custom_call_target="tpu_custom_call" | custom-call | tf_op jit(solution)/shard_map/layer/pallas_call | solution.py:531
  45.9 1.4 %store.1 = (bf16[1,256,256]{2,1,0:T(8,128)(2,1)}, bf16[1,256,256]{2,1,0:T(8,128)(2,1)}, f32[256,256]{1,0:T(8,128)}, f32[256,256]{1,0:T(8,128)}, f32[256,256]{1,0...) custom-call(bf16[1,256,256]{2,1,0:T(8,128)(2,1)S(1)} %get-tuple-element.14.refs_0_, ...), custom_call_target="tpu_custom_call" | custom-call | tf_op jit(solution)/shard_map/store/pallas_call | solution.py:547

commit v5 on v4

--- a/solution.py
+++ b/solution.py
@@ -97,6 +97,9 @@
     cons = mcell.shape[1]
     sector = lax.axis_index("phi")
     ev = lax.axis_index("ev")
+    low, high = lax.rem(ev, 2), ev // 2
+    low_peer = ev + 1 - 2 * low
+    high_peer = ev + 2 - 4 * high
     pending = []
 
     fetches = {}
@@ -119,9 +122,6 @@
     def sector_at(distance):
         return lax.rem(sector + (distance + sectors), sectors)
 
-    def ev_at(distance):
-        return lax.rem(ev + distance, ev_count)
-
     def send(src, dst, **target):
         index = len(pending)
         copy = pltpu.make_async_remote_copy(
@@ -142,7 +142,7 @@
 
     if fused:
         greeted = [{"phi": sector_at(d)} for d in range(1, sectors)]
-        greeted += [{"ev": ev_at(d)} for d in range(1, ev_count)]
+        greeted += [{"ev": high_peer}, {"ev": low_peer}]
     else:
         greeted = [{"phi": sector_at(d)} for d in range(-radius, radius + 1) if d]
     barrier = pltpu.get_barrier_semaphore()
@@ -189,6 +189,7 @@
         return copies
 
     local_jet = lax.broadcasted_iota(jnp.int32, (16, cons), 0)
+    upstreams = to_slots(cot[0], up_out, up_in)
     counted = []
     for w in range(window):
         hit = (local_jet + w * JET_DEV == local_row) & (local_jet < JET_DEV)
@@ -225,7 +226,6 @@
     hidden = (cells[0].astype(F32) + before_act * sigmoid).astype(BF16)
     slope = sigmoid * (1.0 + before_act * (1.0 - sigmoid))
     features = to_slots(hidden, feat_out, feat_in)
-    upstreams = to_slots(cot[0], up_out, up_in)
     member_gathered = to_slots(gathered, gath_out, gath_in)
 
     bare = jnp.sum(cell_hot.astype(F32), axis=1, keepdims=True) < 0.5
@@ -316,48 +316,55 @@
 
     def put(values, buffers):
         ref = buffers[0]
-        flat = ref.shape[2]
+        flat = ref.shape[3]
         piece = math.gcd(flat, channels)
-        for e in range(ev_count):
-            for p in range(sectors):
-                for row in range(0, flat, piece):
-                    first = (e * sectors + p) * flat + row
-                    value = values[first // channels]
-                    first = first % channels
-                    ref[e, p, row : row + piece] = value[first : first + piece].astype(BF16)
+        for c in range(2):
+            for x in range(2):
+                for p in range(sectors):
+                    for row in range(0, flat, piece):
+                        first = ((c * 2 + x) * sectors + p) * flat + row
+                        value = values[first // channels]
+                        first = first % channels
+                        ref[c, x, p, row : row + piece] = value[first : first + piece].astype(BF16)
+        return [send(ref.at[1 - low], buffers[1], ev=low_peer)]
+
+    def half(buffers, copies):
+        whole, from_low, middle, from_high = buffers[:4]
+        landed(copies)
+        middle[...] = (whole[low].astype(F32) + from_low[...].astype(F32)).astype(BF16)
+        return [send(middle.at[1 - high], from_high, ev=high_peer)]
+
+    def quarter(buffers, copies):
+        middle, from_high, share, from_phi = buffers[2:6]
+        landed(copies)
+        share[...] = (middle[high].astype(F32) + from_high[...].astype(F32)).astype(BF16)
         return [
-            send(ref.at[ev_at(d)], buffers[1].at[d - 1], ev=ev_at(d)) for d in range(1, ev_count)
-        ]
-
-    def share_phi(buffers, copies):
-        whole, from_ev, middle, from_phi = buffers[:4]
-        landed(copies)
-        total = whole[ev].astype(F32)
-        for d in range(1, ev_count):
-            total = total + from_ev[d - 1].astype(F32)
-        middle[...] = total.astype(BF16)
-        return [
-            send(middle.at[sector_at(d)], from_phi.at[d - 1], phi=sector_at(d))
+            send(share.at[sector_at(d)], from_phi.at[d - 1], phi=sector_at(d))
             for d in range(1, sectors)
         ]
 
     def own_total(buffers, copies):
-        middle, from_phi, final = buffers[2:]
+        share, from_phi, final = buffers[4:]
         landed(copies)
-        total = middle[sector].astype(F32)
+        total = share[sector].astype(F32)
         for d in range(1, sectors):
             total = total + from_phi[d - 1].astype(F32)
-        final[ev, sector] = total.astype(BF16)
-        block = final.at[ev, sector]
+        final[low, high, sector] = total.astype(BF16)
+        block = final.at[low, high, sector]
         return [send(block, block, phi=sector_at(d)) for d in range(1, sectors)]
 
-    def back_ev(buffers, copies):
+    def double(buffers, copies):
         landed(copies)
-        block = buffers[4].at[ev]
-        return [send(block, block, ev=ev_at(d)) for d in range(1, ev_count)]
-
-    if fused:
-        early, late = sums[:5], sums[5:]
+        block = buffers[6].at[low, high]
+        return [send(block, block, ev=high_peer)]
+
+    def redouble(buffers, copies):
+        landed(copies)
+        block = buffers[6].at[low]
+        return [send(block, block, ev=low_peer)]
+
+    if fused:
+        early, late = sums[:7], sums[7:]
 
     landed(upstreams)
     upstream = by_jet(up_in)
@@ -384,7 +391,7 @@
     grad_members = nt(grad_queries, wq[...]) + nt(grad_keys, wk[...]) + nt(grad_vals, wv[...])
     returned = back(grad_members, gmem_out, gmem_in)
     if fused:
-        early_copies = share_phi(early, early_copies)
+        early_copies = half(early, early_copies)
 
     query_term = tn(members, grad_queries)
     key_term = tn(members, grad_keys)
@@ -397,14 +404,15 @@
     message_term = bare_term + tn(rows_gathered, (rows_grad * rows_slope).astype(BF16))
     if fused:
         late_copies = put([query_term, key_term, message_term], late)
-        early_copies = own_total(early, early_copies)
+        early_copies = quarter(early, early_copies)
+        late_copies = half(late, late_copies)
 
     landed(attended)
     all_rows = att_in[...].reshape(window * rows, channels)
     out_cells[0] = (hidden.astype(F32) + nn(cell_slot, all_rows)).astype(BF16)
     if fused:
-        late_copies = share_phi(late, late_copies)
-        early_copies = back_ev(early, early_copies)
+        early_copies = own_total(early, early_copies)
+        late_copies = quarter(late, late_copies)
     landed(returned)
     all_rows = gmem_in[...].reshape(window * rows, channels)
     grad_hidden = cot[0].astype(F32) + nn(cell_slot, all_rows)
@@ -422,7 +430,9 @@
         send(gedge_out.at[1], gedge_in.at[1], phi=sector_at(-1)),
     ]
     if fused:
+        early_copies = double(early, early_copies)
         late_copies = own_total(late, late_copies)
+        early_copies = redouble(early, early_copies)
     landed(grad_edges)
     for b in range(blocks):
         own = slice(b * BLOCK, (b + 1) * BLOCK)
@@ -434,10 +444,11 @@
         grad_cells[0, own] = block.astype(BF16)
 
     if fused:
-        late_copies = back_ev(late, late_copies)
+        late_copies = double(late, late_copies)
+        late_copies = redouble(late, late_copies)
         landed(early_copies + late_copies)
         squares = jnp.zeros((1, channels), F32)
-        blocks_of = [(e, p) for e in range(ev_count) for p in range(sectors)]
+        blocks_of = [(c, x, p) for c in range(2) for x in range(2) for p in range(sectors)]
         for buffers in (early, late):
             for place in blocks_of:
                 value = buffers[-1][place].astype(F32)
@@ -449,7 +460,7 @@
             (early, [grad_value, grad_output]),
             (late, [grad_query, grad_key, grad_message]),
         ):
-            flat = buffers[-1].shape[2]
+            flat = buffers[-1].shape[3]
             piece = math.gcd(flat, channels)
             for index, place in enumerate(blocks_of):
                 block = buffers[-1][place].astype(F32) * factor
@@ -495,7 +506,7 @@
     capacity = -(-capacity // 8) * 8
     rows = JET_DEV * capacity
     shares = sectors * ev_count
-    fused = channels % (16 * shares) == 0
+    fused = ev_count == 4 and channels % (16 * shares) == 0
     copies = 4 + 6 * (window - 1)
     weight = (channels, channels)
     scratch = [pltpu.VMEM(cell_feats.shape, BF16) for _ in range(2)]
@@ -509,9 +520,9 @@
     scratch += [pltpu.VMEM((window, rows, channels), BF16) for _ in range(6)]
     sums = []
     if fused:
-        copies += 4 * (ev_count - 1) + 4 * (sectors - 1)
-        leads = [(ev_count, sectors), (ev_count - 1, sectors), (sectors,), (sectors - 1,)]
-        leads += [(ev_count, sectors)]
+        copies += 2 * (4 + 2 * (sectors - 1))
+        leads = [(2, 2, sectors), (2, sectors), (2, sectors), (sectors,), (sectors,)]
+        leads += [(sectors - 1,), (2, 2, sectors)]
         for count in (2, 3):
             flat = count * channels // shares
             sums += [pltpu.VMEM(lead + (flat, channels), BF16) for lead in leads]

time: 47.4 us -> 46.5 us (0.981)
  Pallas kernels: 46.6 us -> 45.7 us
    pallas_call x1, Pallas kernels: 45.3 us -> 44.3 us  [on_device(): pl.pallas_call(functools.partial(layer_kernel, (sectors, ev_count, radius...]
where the time goes in v5:
time: 46.5 us; the launch traced here: 46.3 us
  Pallas kernels  45.7 us (98%)
  between operations  0.64 us (1%)
    pallas_call x1, Pallas kernels, on_device(): pl.pallas_call(functools.partial(layer_kernel, (sectors, ev_count, radius...  44.3 us
    pallas_call x1, Pallas kernels, on_device(): pl.pallas_call(store_kernel, out_shape=[jax.ShapeDtypeStruct(out.shape, o...  1.37 us

profile of v5, /device:TPU:1, one launch (start us, length us, event | category | flops | bytes accessed | tf_op | source)
XLA Modules:
  0.0 46.3 jit_solution(9045535394788164693)
XLA Ops:
  0.6 44.3 %layer.1 = (bf16[1,256,256]{2,1,0:T(8,128)(2,1)S(1)}, bf16[1,256,256]{2,1,0:T(8,128)(2,1)S(1)}, f32[256,256]{1,0:T(8,128)S(1)}, f32[256,256]{1,0:T(8,128)S(1)}, ...) custom-call(bf16[1,256,256]{2,1,0:T(8,128)(2,1)} %cells_far.1, s32[1,2,4]{2,1,0:T(2,128)} %nbrs_far.1, ...), custom_call_target="tpu_custom_call" | custom-call | tf_op jit(solution)/shard_map/layer/pallas_call | solution.py:542
  45.0 1.4 %store.1 = (bf16[1,256,256]{2,1,0:T(8,128)(2,1)}, bf16[1,256,256]{2,1,0:T(8,128)(2,1)}, f32[256,256]{1,0:T(8,128)}, f32[256,256]{1,0:T(8,128)}, f32[256,256]{1,0...) custom-call(bf16[1,256,256]{2,1,0:T(8,128)(2,1)S(1)} %get-tuple-element.14.refs_0_, ...), custom_call_target="tpu_custom_call" | custom-call | tf_op jit(solution)/shard_map/store/pallas_call | solution.py:558
